TPU v7x, 32 devices: a whole 2x2x4 slice. The times are simulated.
32 devices in a mesh: dp: 2 (over x), expert: 16 (over z, y, core).
Axes of the slice: x: 2, y: 2, z: 4, core: 2. Of those that a mesh axis runs over, the one named last changes fastest.
Arguments:
- tokens: bfloat16 [128, 5120], P(('dp', 'expert')), may hold values from -6 to 6
- chosen_expert_index: int32 [128, 6], P(('dp', 'expert')), may hold values from 0 to 15, all different within a row; in each aligned block of 4 rows (0 to 3, 4 to 7, ...) at most 3 rows name the same one
- router_gate_weight: float32 [128, 6], P(('dp', 'expert')), may hold values from 0.05 to 0.5
- partner: int32 [128], P(('dp', 'expert')), may hold values from 0 to 3, as said below
- gate_up_weight: bfloat16 [16, 2, 1536, 5120], P('expert', None, 'dp'), may hold values from -0.078125 to 0.078125
- adapter_down_weight: bfloat16 [16, 8, 1536], P('expert', None, 'dp'), may hold values from -0.15625 to 0.15625
- adapter_up_weight: bfloat16 [16, 8, 5120], P('expert', None, 'dp'), may hold values from -2 to 2
Outputs:
- down_factor_gradient: float32 [16, 8, 1536], P('expert', None, 'dp')
- up_factor_gradient: float32 [16, 8, 5120], P('expert', None, 'dp')
Inputs may be any that keep to these rules, and one draw needn't show every extreme that they name: `chosen_expert_index`: in each aligned block of 4 rows (the tokens of one device) a token names 6 different experts, no expert is named by more than 3 rows, a bound that some block reaches. Tokens are paired within each aligned block of 4 rows: partner holds the index of the other token of the pair within the block, never the token itself, and partner of partner is the token.
All inputs are finite; a program needn't handle non-finite values.
Results may differ from a plain program's by a relative error of at most 0.0039.
Values may be sent and summed in bfloat16 or wider, within the bound.
No kernel may reach another device: no remote copies, remote signals or barrier semaphores. Data moves between devices by JAX's collectives and lax.ppermute only.
A program may use at most 64 MiB of HBM per device.

v0:
```python
import math

import jax
import jax.numpy as jnp
from jax import lax
from jax.sharding import PartitionSpec as P

adapter_scale = 2.0
control = 0.5
highest_precision = lax.Precision.HIGHEST


def route_tables(chosen_expert_index, router_gate_weight, experts, capacity):
    tok_count, choices = chosen_expert_index.shape
    picks = (chosen_expert_index[:, :, None] == jnp.arange(experts, dtype=jnp.int32)).astype(
        jnp.int32
    )
    flat = picks.reshape(tok_count * choices, experts)
    before = jnp.cumsum(flat, axis=0) - flat
    slots = jnp.sum(before * flat, axis=1).reshape(tok_count, choices)
    places = (slots[:, :, None] == jnp.arange(capacity, dtype=jnp.int32)).astype(jnp.float32)
    chosen = picks.astype(jnp.float32)
    select = jnp.einsum("tke,tkc->ect", chosen, places, precision=highest_precision)
    weighted = jnp.einsum(
        "tke,tkc,tk->ect", chosen, places, router_gate_weight, precision=highest_precision
    )
    return (select.astype(jnp.bfloat16), weighted)


def expert_hidden(rows, w_local):
    flat_rows = rows.reshape(-1, rows.shape[-1])
    both = jnp.einsum("gfd,nd->gfn", w_local, flat_rows, preferred_element_type=jnp.float32)
    return (jax.nn.silu(both[0]) * both[1]).astype(jnp.bfloat16)


def body(
    tokens,
    chosen_expert_index,
    router_gate_weight,
    partner,
    gate_up_weight,
    adapter_down_weight,
    adapter_up_weight,
):
    tok_count, width = tokens.shape
    choices = chosen_expert_index.shape[1]
    groups = lax.axis_size("dp")
    experts = lax.axis_size("expert")
    capacity = min(tok_count, max(2, (2 * tok_count * choices + experts - 1) // experts))
    select, weighted = route_tables(chosen_expert_index, router_gate_weight, experts, capacity)
    w_local = gate_up_weight[0]
    down_factor = adapter_down_weight[0]
    up_factor = adapter_up_weight[0]
    slice_width = up_factor.shape[1]
    outgoing = jnp.einsum("ect,td->ecd", select, tokens, preferred_element_type=jnp.float32).astype(
        jnp.bfloat16
    )
    arrived = lax.all_to_all(outgoing[None], "expert", split_axis=1, concat_axis=1, tiled=True)
    hidden_state = expert_hidden(lax.all_gather(arrived, "dp", axis=0, tiled=True), w_local)
    grid = (groups, experts, capacity)
    partial_low = jnp.einsum(
        "fn,rf->nr", hidden_state, down_factor, preferred_element_type=jnp.float32
    )
    narrow_product = lax.psum(partial_low, "dp")
    delta_flat = (
        adapter_scale
        * jnp.einsum(
            "hy,ya->ha", narrow_product, up_factor.astype(jnp.float32), precision=highest_precision
        )
    ).astype(jnp.bfloat16)
    change_rows = delta_flat.reshape(grid + (slice_width,))
    returned = lax.all_to_all(
        lax.all_to_all(change_rows, "dp", split_axis=0, concat_axis=3, tiled=True),
        "expert",
        split_axis=1,
        concat_axis=1,
        tiled=True,
    )
    returned = returned.reshape(experts, capacity, width)
    delta = jnp.einsum(
        "ect,ecd->td", weighted, returned.astype(jnp.float32), precision=highest_precision
    )
    total = tok_count * groups * experts
    mates = jnp.take(tokens, partner, axis=0).astype(jnp.float32)
    direction = tokens.astype(jnp.float32) - mates
    cotangent = 2.0 / math.sqrt(total) * (delta - control * direction)
    cot_rows = jnp.einsum("ect,td->ecd", weighted, cotangent, precision=highest_precision).astype(
        jnp.bfloat16
    )
    sectioned = cot_rows.reshape(1, experts, capacity, groups, slice_width)
    cot_in = lax.all_to_all(
        lax.all_to_all(sectioned, "dp", split_axis=3, concat_axis=0, tiled=True),
        "expert",
        split_axis=1,
        concat_axis=1,
        tiled=True,
    )
    cot_in = cot_in.reshape(-1, slice_width)
    partial_cot = jnp.einsum("nd,rd->nr", cot_in, up_factor, preferred_element_type=jnp.float32)
    cotangent_narrow = lax.psum(partial_cot, "dp")
    up_factor_gradient = adapter_scale * jnp.einsum(
        "nr,nd->rd", narrow_product, cot_in.astype(jnp.float32), precision=highest_precision
    )
    down_factor_gradient = adapter_scale * jnp.einsum(
        "nr,fn->rf", cotangent_narrow, hidden_state.astype(jnp.float32), precision=highest_precision
    )
    return (down_factor_gradient[None], up_factor_gradient[None])


def solution(mesh):
    placed = (
        P(("dp", "expert"), None),
        P(("dp", "expert"), None),
        P(("dp", "expert"), None),
        P(("dp", "expert")),
        P("expert", None, "dp", None),
        P("expert", None, "dp"),
        P("expert", None, "dp"),
    )
    return jax.shard_map(
        body,
        mesh=mesh,
        in_specs=placed,
        out_specs=(P("expert", None, "dp"), P("expert", None, "dp")),
        check_vma=False,
    )
```

profile of v0, /device:TPU:0, one launch (start us, length us, event | category | flops | bytes accessed | tf_op | source)
XLA Modules:
  0.0 132.2 jit_solution(7403713088751701184)
XLA Ops:
  0.7 0.8 eq.37
  1.8 0.9 fusion.12
  2.7 1.1 fusion.2
  3.8 0.4 copy.15
  4.3 25.4 %all_to_all.51 = bf16[1,16,3,5120]{3,2,0,1:T(4,128)(2,1)S(1)} all-to-all(bf16[1,16,3,5120]{3,2,0,1:T(4,128)(2,1)S(1)} %copy.15), channel_id=1, replica_groups=mesh['dp'=2,'expert'=16] {'expert'}, dimensions={1} | all-to-all | bytes 983040 | tf_op jit(solution)/shard_map/all_to_all | solution.py:58
  29.7 0.2 copy.16
  29.9 14.1 %all_gather.3 = bf16[2,16,3,5120]{3,1,2,0:T(8,128)(2,1)S(1)} all-gather(bf16[1,16,3,5120]{3,1,2,0:T(8,128)(2,1)S(1)} %copy.16), channel_id=1, replica_groups=mesh['dp'=2,'expert'=16] {'dp'}, dimensions={0}, use_global_device_ids=true | all-gather | bytes 1474560 | tf_op jit(solution)/shard_map/all_gather | solution.py:59
  44.0 0.8 copy.17
  44.9 0.9 reshape.45
  45.7 10.4 %fusion.8 = f32[2,768,96]{1,2,0:T(8,128)S(1)} fusion(bf16[96,5120,1]{1,0,2:T(8,128)(2,1)S(1)} %reshape.45, bf16[1,2,768,5120]{3,2,1,0:T(8,128)(2,1)} %param.11), kind=kOutput, calls=%fused_computation.14 | convolution fusion | flops 1509949440 | bytes 17301504 | tf_op jit(solution)/shard_map/gfd,nd->gfn/dot_general | solution.py:32
  56.4 4.9 %psum.14 = f32[96,8]{0,1:T(8,128)S(1)} all-reduce(f32[96,8]{0,1:T(8,128)S(1)} %fusion.19), channel_id=1, replica_groups=mesh['dp'=2,'expert'=16] {'dp'}, use_global_device_ids=true, to_apply=%region_2.3 | all-reduce | flops 768 | bytes 6144 | tf_op jit(solution)/shard_map/psum | solution.py:64
  61.3 0.6 fusion.6
  61.9 0.3 reshape.31
  62.3 9.0 %all_to_all.52 = bf16[2,16,3,2560]{3,1,2,0:T(8,128)(2,1)S(1)} all-to-all(bf16[2,16,3,2560]{3,1,2,0:T(8,128)(2,1)S(1)} %copy.18), channel_id=1, replica_groups=mesh['dp'=2,'expert'=16] {'dp'}, dimensions={0} | all-to-all | bytes 983040 | tf_op jit(solution)/shard_map/all_to_all | solution.py:73
  71.3 0.5 copy.27
  71.8 1.2 reshape.49
  72.9 3.6 %all-to-all-start.2 = ((bf16[1,16,3,5120]{3,2,0,1:T(4,128)(2,1)}), bf16[1,16,3,5120]{3,2,0,1:T(4,128)(2,1)S(1)}, u32[]{:S(2)}, u32[]{:S(2)}) async-start(bf16[1,16,3,5120]{3,2,0,1:T(4,128)(2,1)} %reshape.49), calls=%async_computation.2 | async-start | bytes 1310720 | tf_op jit(solution)/shard_map/all_to_all | solution.py:72
  76.6 0.6 gather_fusion
  77.2 0.2 convolution_bitcast_fusion.1
  77.4 15.7 %all-to-all-done.2 = bf16[1,16,3,5120]{3,2,0,1:T(4,128)(2,1)S(1)} async-done(((bf16[1,16,3,5120]{3,2,0,1:T(4,128)(2,1)}), bf16[1,16,3,5120]{3,2,0,1:T(4,128)(2,1)S(1)}, u32[]{:S(2)}, u32[]{:S(2)}) %all-to-all-start.2) | async-done | bytes 491552 | tf_op jit(solution)/shard_map/all_to_all | solution.py:72
  93.1 0.5 fusion.5
  93.5 1.0 convolution_convert_fusion
  94.6 0.4 reshape.33
  95.0 10.5 %all_to_all.53 = bf16[1,16,3,2,2560]{4,1,2,0,3:T(8,128)(2,1)S(1)} all-to-all(bf16[1,16,3,2,2560]{4,1,2,0,3:T(8,128)(2,1)S(1)} %copy.24), channel_id=1, replica_groups=mesh['dp'=2,'expert'=16] {'dp'}, dimensions={3} | all-to-all | bytes 983040 | tf_op jit(solution)/shard_map/all_to_all | solution.py:92
  105.5 0.5 copy.25
  106.0 18.5 %all_to_all.54 = bf16[2,16,3,1,2560]{4,0,3,2,1:T(2,128)(2,1)S(1)} all-to-all(bf16[2,16,3,1,2560]{4,0,3,2,1:T(2,128)(2,1)S(1)} %copy.25), channel_id=1, replica_groups=mesh['dp'=2,'expert'=16] {'expert'}, dimensions={1} | all-to-all | bytes 983040 | tf_op jit(solution)/shard_map/all_to_all | solution.py:91
  124.5 0.3 copy.26
  124.8 0.4 reshape.34
  125.2 0.9 fusion.7
  126.2 0.2 fusion.22
  126.4 4.9 %psum.15 = f32[96,8]{0,1:T(8,128)S(1)} all-reduce(f32[96,8]{0,1:T(8,128)S(1)} %fusion.22), channel_id=1, replica_groups=mesh['dp'=2,'expert'=16] {'dp'}, use_global_device_ids=true, to_apply=%region_3.4 | all-reduce | flops 768 | bytes 6144 | tf_op jit(solution)/shard_map/psum | solution.py:100
  131.3 0.9 fusion.11
  (22 shorter events, 0.8 us)
Async XLA Ops:
  0.6 60.7 %copy-start = (bf16[1,8,2560]{2,1,0:T(8,128)(2,1)S(1)}, bf16[1,8,2560]{2,1,0:T(8,128)(2,1)}, u32[]{:S(2)}) copy-start(bf16[1,8,2560]{2,1,0:T(8,128)(2,1)} %param.13) | copy-start | bytes 122884
  0.6 55.5 %copy-start.3 = (bf16[1,8,768]{2,1,0:T(8,128)(2,1)S(1)}, bf16[1,8,768]{2,1,0:T(8,128)(2,1)}, u32[]{:S(2)}) copy-start(bf16[1,8,768]{2,1,0:T(8,128)(2,1)} %param.12) | copy-start | bytes 36868
  44.0 32.5 %copy-start.5 = (s32[4]{0:T(128)S(1)}, s32[4]{0:T(128)}, u32[]{:S(2)}) copy-start(s32[4]{0:T(128)} %param.10) | copy-start | bytes 52
  44.0 32.5 %copy-start.1 = (bf16[4,5120]{1,0:T(4,128)(2,1)S(1)}, bf16[4,5120]{1,0:T(4,128)(2,1)}, u32[]{:S(2)}) copy-start(bf16[4,5120]{1,0:T(4,128)(2,1)} %param.7) | copy-start | bytes 122884
  44.0 33.2 %copy-start.2 = (s32[4,6]{1,0:T(4,128)S(1)}, s32[4,6]{1,0:T(4,128)}, u32[]{:S(2)}) copy-start(s32[4,6]{1,0:T(4,128)} %param.8) | copy-start | bytes 292
  44.0 33.2 %copy-start.4 = (f32[4,6]{1,0:T(4,128)S(1)}, f32[4,6]{1,0:T(4,128)}, u32[]{:S(2)}) copy-start(f32[4,6]{1,0:T(4,128)} %param.9) | copy-start | bytes 292
  72.9 20.2 %all-to-all-start.2 = ((bf16[1,16,3,5120]{3,2,0,1:T(4,128)(2,1)}), bf16[1,16,3,5120]{3,2,0,1:T(4,128)(2,1)S(1)}, u32[]{:S(2)}, u32[]{:S(2)}) async-start(bf16[1,16,3,5120]{3,2,0,1:T(4,128)(2,1)} %reshape.49), calls=%async_computation.2 | async-start | bytes 1310720 | tf_op jit(solution)/shard_map/all_to_all | solution.py:72
where the time goes:
time: 133 us; the launch traced here: 132 us
  blocking collectives  87.5 us (66%)
  matrix products  16.9 us (13%)
  waiting for transfers between devices  15.7 us (12%)
  local copies, waits for them, and re-layouts  7.42 us (6%)
  starting transfers between devices  3.59 us (3%)
    all_to_all x1, blocking collectives, body(): lax.all_to_all(outgoing[None], 'expert', split_axis=1, concat_axis=1, til...  25.4 us
    all_to_all x1, blocking collectives, body(): lax.all_to_all(lax.all_to_all(sectioned, 'dp', split_axis=3, concat_axis=...  18.5 us
    all_to_all x1, waiting for transfers between devices, body(): lax.all_to_all(lax.all_to_all(change_rows, 'dp', split_axis=0, concat_axi...  15.7 us
    all_gather x1, blocking collectives, body(): lax.all_gather(arrived, 'dp', axis=0, tiled=True)  14.1 us
    all_to_all x1, blocking collectives, body(): lax.all_to_all(sectioned, 'dp', split_axis=3, concat_axis=0, tiled=True)  10.5 us
    dot_general x1, matrix products, expert_hidden(): jnp.einsum('gfd,nd->gfn', w_local, flat_rows, preferred_element_type=jnp....  10.4 us
    all_to_all x1, blocking collectives, body(): lax.all_to_all(change_rows, 'dp', split_axis=0, concat_axis=3, tiled=True)  8.97 us
    psum x1, blocking collectives, body(): cotangent_narrow = lax.psum(partial_cot, 'dp')  4.95 us
  transfers between devices with their start and end apart: 1, of which 1 were waited for; matrix products, arithmetic and copies ran while one was open for 1% of the time, Pallas kernels for 0%

commit v1 on v0

--- a/solution.py
+++ b/solution.py
@@ -1,13 +1,21 @@
+import functools
 import math
 
 import jax
 import jax.numpy as jnp
 from jax import lax
+from jax.experimental import pallas as pl
+from jax.experimental.pallas import tpu as pltpu
+from jax.sharding import Mesh
 from jax.sharding import PartitionSpec as P
 
 adapter_scale = 2.0
 control = 0.5
 highest_precision = lax.Precision.HIGHEST
+f32 = jnp.float32
+bf16 = jnp.bfloat16
+every = ("dp", "chip", "core")
+mib = 1 << 20
 
 
 def route_tables(chosen_expert_index, router_gate_weight, experts, capacity):
@@ -33,7 +41,7 @@
     return (jax.nn.silu(both[0]) * both[1]).astype(jnp.bfloat16)
 
 
-def body(
+def slot_body(
     tokens,
     chosen_expert_index,
     router_gate_weight,
@@ -107,20 +115,303 @@
     return (down_factor_gradient[None], up_factor_gradient[None])
 
 
+def mask_of(block):
+    return (
+        ((block & 1) << 2)
+        | (((block >> 1) & 1) << 3)
+        | (((block >> 2) & 1) << 4)
+        | (((block >> 3) & 1) << 1)
+        | ((block >> 4) & 1)
+    )
+
+
+def own_number():
+    return (lax.axis_index("dp") * lax.axis_size("chip") + lax.axis_index("chip")) * 2 + (
+        lax.axis_index("core")
+    )
+
+
+def dot(left, right, left_dim, right_dim, precision=None):
+    return lax.dot_general(
+        left,
+        right,
+        (((left_dim,), (right_dim,)), ((), ())),
+        precision=precision,
+        preferred_element_type=f32,
+    )
+
+
+def split_two(value):
+    high = value.astype(bf16)
+    return high, (value - high.astype(f32)).astype(bf16)
+
+
+def order_table(count):
+    lane = lax.broadcasted_iota(jnp.int32, (count, count), 1)
+    row = lax.broadcasted_iota(jnp.int32, (count, count), 0)
+    whole = ((mask_of(lane >> 2) ^ own_number()) << 2) | (lane & 3)
+    return (row == whole).astype(f32).astype(bf16)
+
+
+def meta_kernel(index_ref, gate_ref, partner_ref, meta_ref, index_s, gate_s, partner_s, sems):
+    copies = [
+        pltpu.make_async_copy(index_ref, index_s, sems.at[0]),
+        pltpu.make_async_copy(gate_ref, gate_s, sems.at[1]),
+        pltpu.make_async_copy(partner_ref, partner_s, sems.at[2]),
+    ]
+    for copy in copies:
+        copy.start()
+    for copy in copies:
+        copy.wait()
+    lane = lax.broadcasted_iota(jnp.int32, (8, 128), 1)
+    row = lax.broadcasted_iota(jnp.int32, (8, 128), 0)
+    dense = jnp.zeros((8, 128), f32)
+    mates = jnp.zeros((8, 128), f32)
+    for t in range(index_ref.shape[0]):
+        for k in range(index_ref.shape[1]):
+            dense = dense + jnp.where((lane & 63) == index_s[t, k] * 4 + t, gate_s[t, k], 0.0)
+        mates = mates + jnp.where(lane == 64 + t, partner_s[t].astype(f32), 0.0)
+    high = dense.astype(bf16).astype(f32)
+    middle = (dense - high).astype(bf16).astype(f32)
+    low = dense - high - middle
+    first = jnp.where(lane < 64, high, middle)
+    second = jnp.where(lane < 64, low, mates)
+    rows = jnp.where(row == 0, first, jnp.where(row == 1, second, 0.0))
+    meta_ref[...] = jnp.concatenate([jnp.zeros((8, 128), f32), rows], axis=0).astype(bf16)
+
+
+def whole_rows_kernel(own_ref, other_ref, out_ref):
+    half = own_ref.shape[1]
+    at = pl.multiple_of(lax.axis_index("dp") * half, 128)
+    out_ref[:, pl.ds(at, half)] = own_ref[...]
+    at = pl.multiple_of((1 - lax.axis_index("dp")) * half, 128)
+    out_ref[:, pl.ds(at, half)] = other_ref[...]
+
+
+def hidden_kernel(chunks, pieces, *refs):
+    x_refs = refs[:pieces]
+    w_ref, v_ref, up_ref, meta_ref = refs[pieces : pieces + 4]
+    hid_ref, low_ref, cross_ref, send_ref = refs[pieces + 4 : pieces + 8]
+    x_all, w_buf, sems = refs[pieces + 8 :]
+    units = w_ref.shape[1]
+    step = units // chunks
+
+    def fetch(i):
+        return pltpu.make_async_copy(w_ref.at[:, pl.ds(i * step, step), :], w_buf.at[i], sems.at[i])
+
+    ahead = 3
+    for i in range(ahead):
+        fetch(i).start()
+    rows = x_refs[0].shape[0]
+    for p in range(pieces):
+        x_all[pl.ds(p * rows, rows), :] = x_refs[p][...]
+    x = x_all[...]
+    low = jnp.zeros(low_ref.shape, f32)
+    for i in range(chunks):
+        fetch(i).wait()
+        if i + ahead < chunks:
+            fetch(i + ahead).start()
+        gate = dot(w_buf[i, 0], x, 1, 1)
+        up = dot(w_buf[i, 1], x, 1, 1)
+        hidden = (gate / (1.0 + jnp.exp(-gate)) * up).astype(bf16)
+        hid_ref[pl.ds(i * step, step), :] = hidden
+        low = low + dot(v_ref[:, pl.ds(i * step, step)], hidden, 1, 0)
+    low_ref[...] = low
+    cross_ref[...] = dot(up_ref[...], x, 1, 1)
+    ordered = dot(low.astype(bf16), order_table(x.shape[0]), 1, 1)
+    block = jnp.concatenate([ordered, jnp.zeros_like(ordered)], axis=0).astype(bf16)
+    block = block + meta_ref[...]
+    for i in range(send_ref.shape[0]):
+        send_ref[i] = block
+
+
+def gradient_kernel(pieces, *refs):
+    x_refs = refs[:pieces]
+    near_ref, far_ref, up_near, up_far, hid_ref, low_ref, cross_ref = refs[pieces : pieces + 7]
+    down_out, up_out = refs[pieces + 7 : pieces + 9]
+    blocks_buf, wide_buf = refs[pieces + 9 :]
+    tokens = hid_ref.shape[1]
+    blocks = tokens // 4
+    half = up_out.shape[1]
+    dp = lax.axis_index("dp")
+    chip = lax.axis_index("chip")
+    chips = lax.axis_size("chip")
+    at = pl.multiple_of(dp * half, 128)
+    for b in range(blocks):
+        mask = mask_of(b)
+        source = far_ref if mask & 1 else near_ref
+        blocks_buf[b] = source[(dp ^ (mask >> 4)) * chips + (chip ^ ((mask >> 1) & 7))]
+    received = blocks_buf[...]
+    local = dot(received.reshape(blocks * 16, tokens), order_table(tokens), 1, 0)
+    local = local.reshape(4, 2, 4, 16, tokens)[:, :, :, 0:8]
+    lows = (local[:, 0] + local[:, 1]).reshape(16, 8, tokens)
+    own_low = low_ref[...] + local[0, 1, 0]
+
+    lane = lax.broadcasted_iota(jnp.int32, (blocks, tokens), 1)
+    row = lax.broadcasted_iota(jnp.int32, (blocks, tokens), 0)
+    spread = ((lane >> 2) == row).astype(f32).astype(bf16)
+    wide = received.astype(f32)
+    first = dot(wide[:, 8].astype(bf16), spread, 0, 0)
+    second = dot(wide[:, 9].astype(bf16), spread, 0, 0)
+    lane = lax.broadcasted_iota(jnp.int32, (tokens, tokens), 1)
+    row = lax.broadcasted_iota(jnp.int32, (tokens, tokens), 0)
+    same = (row & 3) == (lane & 3)
+    first = jnp.where(same, first, 0.0)
+    second = jnp.where(same, second, 0.0)
+    mate = jnp.sum(second[64:72], axis=0, keepdims=True).astype(jnp.int32)
+    mate = (lax.broadcasted_iota(jnp.int32, (1, tokens), 1) & ~3) | mate
+    k = row >> 3
+    away = ((k & 1) << 2) | (((k >> 1) & 1) << 3) | (((k >> 2) & 1) << 1) | ((k >> 3) & 1)
+    expert = (own_number() & 15) ^ away
+    pick = ((lane >> 2) & 15) == expert
+    pick_first = pick.astype(f32).astype(bf16)
+    pick_second = (pick & (lane < 64)).astype(f32).astype(bf16)
+    gates = dot(pick_first, first.astype(bf16), 1, 0) + dot(pick_second, second.astype(bf16), 1, 0)
+
+    scale = 2.0 / math.sqrt(tokens)
+    weight = scale * gates[0:1]
+    upper = adapter_scale * gates * lows.reshape(tokens, tokens) * weight
+    apart = (row == lane).astype(f32) - (row == mate).astype(f32)
+    lower = -control * apart * weight
+    factors = jnp.concatenate([upper, lower], axis=0)
+
+    whole_up = jnp.concatenate([up_near[...], up_far[...]], axis=0)
+    gram = dot(up_near[0:8, :], whole_up, 1, 1)
+    products = jnp.concatenate([gram, cross_ref[...]], axis=1)
+    cot_low = dot(products, factors, 1, 0, highest_precision)
+    high, low = split_two(adapter_scale * cot_low)
+    down = dot(jnp.concatenate([high, low], axis=0), hid_ref[...], 1, 1)
+    down_out[...] = down[0:8] + down[8:16]
+
+    rows = x_refs[0].shape[0]
+    near_rows = up_near.shape[0]
+    wide_buf[pl.ds(0, near_rows), :] = up_near[:, pl.ds(at, half)]
+    wide_buf[pl.ds(near_rows, near_rows), :] = up_far[:, pl.ds(at, half)]
+    for p in range(pieces):
+        wide_buf[pl.ds(2 * near_rows + p * rows, rows), :] = x_refs[p][:, pl.ds(at, half)]
+    mixed = dot(own_low, factors, 1, 1, highest_precision)
+    high, low = split_two(adapter_scale * mixed)
+    up = dot(jnp.concatenate([high, low], axis=0), wide_buf[...], 1, 0)
+    up_out[...] = up[0:8] + up[8:16]
+
+
+def dense_body(
+    tokens,
+    chosen_expert_index,
+    router_gate_weight,
+    partner,
+    gate_up_weight,
+    adapter_down_weight,
+    adapter_up_weight,
+):
+    tok_count, width = tokens.shape
+    devices = lax.axis_size("dp") * lax.axis_size("chip") * lax.axis_size("core")
+    total = tok_count * devices
+    units = gate_up_weight.shape[2]
+    rank = adapter_up_weight.shape[1]
+    half = adapter_up_weight.shape[2]
+    vmem = pl.BlockSpec(memory_space=pltpu.VMEM)
+    anywhere = pl.BlockSpec(memory_space=pl.ANY)
+
+    def swap(value, mask):
+        return lax.ppermute(value, every, [(i, i ^ mask) for i in range(devices)])
+
+    def grow(value, mask):
+        return jnp.concatenate([value, swap(value, mask)], axis=0)
+
+    meta = pl.pallas_call(
+        meta_kernel,
+        out_shape=jax.ShapeDtypeStruct((16, total), bf16),
+        in_specs=[anywhere] * 3,
+        out_specs=vmem,
+        scratch_shapes=[
+            pltpu.SMEM(chosen_expert_index.shape, jnp.int32),
+            pltpu.SMEM(router_gate_weight.shape, f32),
+            pltpu.SMEM(partner.shape, jnp.int32),
+            pltpu.SemaphoreType.DMA((3,)),
+        ],
+        name="meta",
+    )(chosen_expert_index, router_gate_weight, partner)
+
+    column = grow(grow(tokens, 4), 8)
+    near = [column, swap(column, 16), swap(column, 2), swap(column, 18)]
+    pieces = near + [swap(piece, 1) for piece in near]
+
+    own_up = adapter_up_weight[0]
+    whole_up = pl.pallas_call(
+        whole_rows_kernel,
+        out_shape=jax.ShapeDtypeStruct((rank, width), bf16),
+        in_specs=[vmem, vmem],
+        out_specs=vmem,
+        name="whole_rows",
+    )(own_up, swap(own_up, 16))
+    up_near = grow(grow(grow(whole_up, 4), 8), 2)
+    up_far = swap(up_near, 1)
+
+    chunks = 6
+    count = len(pieces)
+    hidden, low, cross, send = pl.pallas_call(
+        functools.partial(hidden_kernel, chunks, count),
+        out_shape=(
+            jax.ShapeDtypeStruct((units, total), bf16),
+            jax.ShapeDtypeStruct((rank, total), f32),
+            jax.ShapeDtypeStruct((rank, total), f32),
+            jax.ShapeDtypeStruct((devices // 2, 16, total), bf16),
+        ),
+        in_specs=[vmem] * count + [anywhere] + [vmem] * 3,
+        out_specs=(vmem,) * 4,
+        scratch_shapes=[
+            pltpu.VMEM((total, width), bf16),
+            pltpu.VMEM((chunks, 2, units // chunks, width), bf16),
+            pltpu.SemaphoreType.DMA((chunks,)),
+        ],
+        compiler_params=pltpu.CompilerParams(vmem_limit_bytes=40 * mib),
+        name="hidden",
+    )(*pieces, gate_up_weight[0], adapter_down_weight[0], whole_up, meta)
+
+    from_near = lax.all_to_all(send, ("dp", "chip"), split_axis=0, concat_axis=0, tiled=True)
+    from_far = swap(from_near, 1)
+
+    down, up = pl.pallas_call(
+        functools.partial(gradient_kernel, count),
+        out_shape=(
+            jax.ShapeDtypeStruct((rank, units), f32),
+            jax.ShapeDtypeStruct((rank, half), f32),
+        ),
+        in_specs=[vmem] * (count + 7),
+        out_specs=(vmem, vmem),
+        scratch_shapes=[
+            pltpu.VMEM((devices, 16, total), bf16),
+            pltpu.VMEM((2 * total, half), bf16),
+        ],
+        compiler_params=pltpu.CompilerParams(vmem_limit_bytes=32 * mib),
+        name="gradient",
+    )(*pieces, from_near, from_far, up_near, up_far, hidden, low, cross)
+    return (down[None], up[None])
+
+
 def solution(mesh):
+    groups, experts = mesh.shape["dp"], mesh.shape["expert"]
+    if (groups, experts) == (2, 16):
+        cut = Mesh(mesh.devices.reshape(groups, experts // 2, 2), every)
+        data, owners = every, ("chip", "core")
+        run, mesh = dense_body, cut
+    else:
+        data, owners = ("dp", "expert"), "expert"
+        run = slot_body
     placed = (
-        P(("dp", "expert"), None),
-        P(("dp", "expert"), None),
-        P(("dp", "expert"), None),
-        P(("dp", "expert")),
-        P("expert", None, "dp", None),
-        P("expert", None, "dp"),
-        P("expert", None, "dp"),
+        P(data, None),
+        P(data, None),
+        P(data, None),
+        P(data),
+        P(owners, None, "dp", None),
+        P(owners, None, "dp"),
+        P(owners, None, "dp"),
     )
     return jax.shard_map(
-        body,
+        run,
         mesh=mesh,
         in_specs=placed,
-        out_specs=(P("expert", None, "dp"), P("expert", None, "dp")),
+        out_specs=(P(owners, None, "dp"), P(owners, None, "dp")),
         check_vma=False,
     )

time: 133 us -> 70.4 us (0.53)
  blocking collectives: 87.5 us -> 13.4 us
  matrix products: 16.9 us -> 0 us
  Pallas kernels: 0 us -> 13.2 us
  starting transfers between devices: 3.59 us -> 16.4 us
  local copies, waits for them, and re-layouts: 7.42 us -> 1.31 us
  waiting for transfers between devices: 15.7 us -> 21.3 us
  other arithmetic: 0.32 us -> 3.63 us
    all_to_all x4 -> x1, blocking collectives: 63.5 us -> 13.4 us  [dense_body(): lax.all_to_all(send, ('dp', 'chip'), split_axis=0, concat_axis=0, tiled=T...]
    ppermute x0 -> x15, waiting for transfers between devices: none -> 21.3 us  [swap(): return lax.ppermute(value, every, [(i, i ^ mask) for i in range(devices)])]
    dot_general x11 -> x0, matrix products: 16.9 us -> none  [the longest x1 10.4 us: expert_hidden(): jnp.einsum('gfd,nd->gfn', w_local, flat_rows, preferred_element_type=jnp....]
    ppermute x0 -> x15, starting transfers between devices: none -> 16.4 us  [swap(): return lax.ppermute(value, every, [(i, i ^ mask) for i in range(devices)])]
    all_to_all x1 -> x0, waiting for transfers between devices: 15.7 us -> none  [body(): lax.all_to_all(lax.all_to_all(change_rows, 'dp', split_axis=0, concat_axi...]
    all_gather x1 -> x0, blocking collectives: 14.1 us -> none  [body(): lax.all_gather(arrived, 'dp', axis=0, tiled=True)]
    pallas_call x0 -> x4, Pallas kernels: none -> 13.2 us  [the longest x1 7.83 us: dense_body(): pl.pallas_call(functools.partial(hidden_kernel, chunks, count), out_shape...]
    psum x2 -> x0, blocking collectives: 9.88 us -> none  [the longest x1 4.95 us: body(): cotangent_narrow = lax.psum(partial_cot, 'dp')]
  transfers between devices with their start and end apart: 1 -> 15, of which waited for: 1 -> 9; matrix products, arithmetic and copies ran while one was open for 1% -> 4% of each run, Pallas kernels for 0% -> 13%
where the time goes in v1:
time: 70.4 us; the launch traced here: 70 us
  waiting for transfers between devices  21.3 us (30%)
  starting transfers between devices  16.4 us (23%)
  blocking collectives  13.4 us (19%)
  Pallas kernels  13.2 us (19%)
  other arithmetic  3.63 us (5%)
  local copies, waits for them, and re-layouts  1.31 us (2%)
  between operations  0.76 us (1%)
    ppermute x15, waiting for transfers between devices, swap(): return lax.ppermute(value, every, [(i, i ^ mask) for i in range(devices)])  21.3 us
    ppermute x15, starting transfers between devices, swap(): return lax.ppermute(value, every, [(i, i ^ mask) for i in range(devices)])  16.4 us
    all_to_all x1, blocking collectives, dense_body(): lax.all_to_all(send, ('dp', 'chip'), split_axis=0, concat_axis=0, tiled=T...  13.4 us
    pallas_call x1, Pallas kernels, dense_body(): pl.pallas_call(functools.partial(hidden_kernel, chunks, count), out_shape...  7.83 us
    concatenate x5, other arithmetic, grow(): return jnp.concatenate([value, swap(value, mask)], axis=0)  3.63 us
    pallas_call x1, Pallas kernels, dense_body(): pl.pallas_call(functools.partial(gradient_kernel, count), out_shape=(jax....  2.51 us
    pallas_call x1, Pallas kernels, dense_body(): pl.pallas_call(whole_rows_kernel, out_shape=jax.ShapeDtypeStruct((rank, w...  1.44 us
  transfers between devices with their start and end apart: 15, of which 9 were waited for; matrix products, arithmetic and copies ran while one was open for 4% of the time, Pallas kernels for 13%

profile of v1, /device:TPU:0, one launch (start us, length us, event | category | flops | bytes accessed | tf_op | source)
XLA Modules:
  0.0 70.0 jit_solution(17491333070312893458)
XLA Ops:
  0.6 3.0 %collective-permute-start.9 = (bf16[8,2560]{1,0:T(8,128)(2,1)}, bf16[8,2560]{1,0:T(8,128)(2,1)S(1)}, u32[]{:S(2)}, u32[]{:S(2)}) collective-permute-start(bf16[8,2560]{1,0:T(8,128)(2,1)} %bitcast.7), channel_id=1, source_target_pairs={{0,16},{1,17},{2,18},{3,19},{4,20},{5,21},{6,22},{7,23},{8,24},{9,... | collective-permute-start | bytes 122888 | tf_op jit(solution)/shard_map/ppermute | solution.py:317
  3.6 2.2 %collective-permute-done.9.other_ref = bf16[8,2560]{1,0:T(8,128)(2,1)S(1)} collective-permute-done((bf16[8,2560]{1,0:T(8,128)(2,1)}, bf16[8,2560]{1,0:T(8,128)(2,1)S(1)}, u32[]{:S(2)}, u32[]{:S(2)}) %collective-permute-start.9) | collective-permute-done | bytes 40992 | tf_op jit(solution)/shard_map/ppermute | solution.py:317
  5.8 0.6 copy-done.4
  6.4 1.4 %whole_rows.1.refs_10_ = bf16[8,5120]{1,0:T(8,128)(2,1)} custom-call(bf16[8,2560]{1,0:T(8,128)(2,1)} %bitcast.8, bf16[8,2560]{1,0:T(8,128)(2,1)} %copy-done.4), custom_call_target="tpu_custom_call" | custom-call | tf_op jit(solution)/shard_map/whole_rows/pallas_call | solution.py:341
  7.9 2.1 %collective-permute-start.11 = (bf16[8,5120]{1,0:T(8,128)(2,1)}, bf16[8,5120]{1,0:T(8,128)(2,1)S(1)}, u32[]{:S(2)}, u32[]{:S(2)}) collective-permute-start(bf16[8,5120]{1,0:T(8,128)(2,1)} %whole_rows.1.refs_10_), channel_id=1, source_target_pairs={{0,4},{1,5},{2,6},{3,7},{4,0},{5,1},{6,2},{7,3},{8,12},{9,13},{10,... | collective-permute-start | bytes 245768 | tf_op jit(solution)/shard_map/ppermute | solution.py:317
  10.0 2.6 %collective-permute-done.11 = bf16[8,5120]{1,0:T(8,128)(2,1)S(1)} collective-permute-done((bf16[8,5120]{1,0:T(8,128)(2,1)}, bf16[8,5120]{1,0:T(8,128)(2,1)S(1)}, u32[]{:S(2)}, u32[]{:S(2)}) %collective-permute-start.11) | collective-permute-done | bytes 81952 | tf_op jit(solution)/shard_map/ppermute | solution.py:317
  12.6 0.9 %pad_maximum_fusion.3 = bf16[16,5120]{1,0:T(8,128)(2,1)S(1)} fusion(bf16[8,5120]{1,0:T(8,128)(2,1)S(1)} %collective-permute-done.11, bf16[8,5120]{1,0:T(8,128)(2,1)} %whole_rows.1.refs_10_), kind=kLoop, calls=%fused_computation.3 | loop fusion | flops 327680 | bytes 327680 | tf_op jit(solution)/shard_map/concatenate | solution.py:320
  13.5 3.1 %collective-permute-start.12 = (bf16[16,5120]{1,0:T(8,128)(2,1)S(1)}, bf16[16,5120]{1,0:T(8,128)(2,1)S(1)}, u32[]{:S(2)}, u32[]{:S(2)}) collective-permute-start(bf16[16,5120]{1,0:T(8,128)(2,1)S(1)} %pad_maximum_fusion.3), channel_id=1, source_target_pairs={{0,8},{1,9},{2,10},{3,11},{4,12},{5,13},{6,14},{7,15},{8,0},{9,1},... | collective-permute-start | bytes 491528 | tf_op jit(solution)/shard_map/ppermute | solution.py:317
  16.6 1.6 %collective-permute-start = (bf16[4,5120]{1,0:T(4,128)(2,1)}, bf16[4,5120]{1,0:T(4,128)(2,1)S(1)}, u32[]{:S(2)}, u32[]{:S(2)}) collective-permute-start(bf16[4,5120]{1,0:T(4,128)(2,1)} %param.7), channel_id=1, source_target_pairs={{0,4},{1,5},{2,6},{3,7},{4,0},{5,1},{6,2},{7,3},{8,12},{9,13},{10,... | collective-permute-start | bytes 122888 | tf_op jit(solution)/shard_map/ppermute | solution.py:317
  18.2 3.8 %collective-permute-done.12 = bf16[16,5120]{1,0:T(8,128)(2,1)S(1)} collective-permute-done((bf16[16,5120]{1,0:T(8,128)(2,1)S(1)}, bf16[16,5120]{1,0:T(8,128)(2,1)S(1)}, u32[]{:S(2)}, u32[]{:S(2)}) %collective-permute-start.12) | collective-permute-done | bytes 163872 | tf_op jit(solution)/shard_map/ppermute | solution.py:317
  22.1 0.9 %pad_maximum_fusion.1 = bf16[32,5120]{1,0:T(8,128)(2,1)S(1)} fusion(bf16[16,5120]{1,0:T(8,128)(2,1)S(1)} %collective-permute-done.12, bf16[8,5120]{1,0:T(8,128)(2,1)S(1)} %collective-permute-done.11, bf16[8,5120]{1,0:T(8,128)(2,1)} %whole_rows.1.refs_10_), kind=kLoop, calls=%fused_computation.1 | loop fusion | flops 983040 | bytes 655360 | tf_op jit(solution)/shard_map/concatenate | solution.py:320
  23.0 1.6 %collective-permute-start.13 = (bf16[32,5120]{1,0:T(8,128)(2,1)S(1)}, bf16[32,5120]{1,0:T(8,128)(2,1)S(1)}, u32[]{:S(2)}, u32[]{:S(2)}) collective-permute-start(bf16[32,5120]{1,0:T(8,128)(2,1)S(1)} %pad_maximum_fusion.1), channel_id=1, source_target_pairs={{0,2},{1,3},{2,0},{3,1},{4,6},{5,7},{6,4},{7,5},{8,10},{9,11},{10,... | collective-permute-start | bytes 983048 | tf_op jit(solution)/shard_map/ppermute | solution.py:317
  24.6 0.8 %pad_maximum_fusion.4 = bf16[8,5120]{1,0:T(8,128)(2,1)S(1)} fusion(bf16[4,5120]{1,0:T(4,128)(2,1)S(1)} %collective-permute-done, bf16[4,5120]{1,0:T(4,128)(2,1)} %param.7), kind=kLoop, calls=%fused_computation.4 | loop fusion | flops 163840 | bytes 163840 | tf_op jit(solution)/shard_map/concatenate | solution.py:320
  25.4 0.9 %collective-permute-start.1 = (bf16[8,5120]{1,0:T(8,128)(2,1)S(1)}, bf16[8,5120]{1,0:T(8,128)(2,1)S(1)}, u32[]{:S(2)}, u32[]{:S(2)}) collective-permute-start(bf16[8,5120]{1,0:T(8,128)(2,1)S(1)} %pad_maximum_fusion.4), channel_id=1, source_target_pairs={{0,8},{1,9},{2,10},{3,11},{4,12},{5,13},{6,14},{7,15},{8,0},{9,1},... | collective-permute-start | bytes 245768 | tf_op jit(solution)/shard_map/ppermute | solution.py:317
  26.4 3.8 %collective-permute-done.13 = bf16[32,5120]{1,0:T(8,128)(2,1)S(1)} collective-permute-done((bf16[32,5120]{1,0:T(8,128)(2,1)S(1)}, bf16[32,5120]{1,0:T(8,128)(2,1)S(1)}, u32[]{:S(2)}, u32[]{:S(2)}) %collective-permute-start.13) | collective-permute-done | bytes 327712 | tf_op jit(solution)/shard_map/ppermute | solution.py:317
  30.1 0.9 %pad_maximum_fusion.refs_10_ = bf16[64,5120]{1,0:T(8,128)(2,1)S(1)} fusion(bf16[32,5120]{1,0:T(8,128)(2,1)S(1)} %collective-permute-done.13, bf16[16,5120]{1,0:T(8,128)(2,1)S(1)} %collective-permute-done.12, bf16[8,5120]{1,0:T(8,128)(2,1)S(1)} %collective-permute-done.11, bf16[8,5120]{1,0:T(8,128)(2,1)} %whole_rows.1.refs_10_), kind=kLoop, calls=%fused_computation | loop fusion | flops 2621440 | bytes 1310720 | tf_op jit(solution)/shard_map/concatenate | solution.py:320
  31.0 0.1 collective-permute-start.14
  31.1 0.6 collective-permute-done.1
  31.7 0.1 pad_maximum_fusion.2.refs_0_
  31.8 2.0 %collective-permute-start.4 = (bf16[16,5120]{1,0:T(8,128)(2,1)S(1)}, bf16[16,5120]{1,0:T(8,128)(2,1)S(1)}, u32[]{:S(2)}, u32[]{:S(2)}) collective-permute-start(bf16[16,5120]{1,0:T(8,128)(2,1)S(1)} %pad_maximum_fusion.2.refs_0_), channel_id=1, source_target_pairs={{0,18},{1,19},{2,16},{3,17},{4,22},{5,23},{6,20},{7,21},{8,26},{9,... | collective-permute-start | bytes 491528 | tf_op jit(solution)/shard_map/ppermute | solution.py:317
  33.8 1.0 %collective-permute-start.3 = (bf16[16,5120]{1,0:T(8,128)(2,1)S(1)}, bf16[16,5120]{1,0:T(8,128)(2,1)S(1)}, u32[]{:S(2)}, u32[]{:S(2)}) collective-permute-start(bf16[16,5120]{1,0:T(8,128)(2,1)S(1)} %pad_maximum_fusion.2.refs_0_), channel_id=1, source_target_pairs={{0,2},{1,3},{2,0},{3,1},{4,6},{5,7},{6,4},{7,5},{8,10},{9,11},{10,... | collective-permute-start | bytes 491528 | tf_op jit(solution)/shard_map/ppermute | solution.py:317
  34.8 0.5 collective-permute-start.2
  35.4 4.4 %collective-permute-done.4.refs_3_ = bf16[16,5120]{1,0:T(8,128)(2,1)S(1)} collective-permute-done((bf16[16,5120]{1,0:T(8,128)(2,1)S(1)}, bf16[16,5120]{1,0:T(8,128)(2,1)S(1)}, u32[]{:S(2)}, u32[]{:S(2)}) %collective-permute-start.4) | collective-permute-done | bytes 163872 | tf_op jit(solution)/shard_map/ppermute | solution.py:317
  39.7 2.6 %collective-permute-done.3.refs_2_ = bf16[16,5120]{1,0:T(8,128)(2,1)S(1)} collective-permute-done((bf16[16,5120]{1,0:T(8,128)(2,1)S(1)}, bf16[16,5120]{1,0:T(8,128)(2,1)S(1)}, u32[]{:S(2)}, u32[]{:S(2)}) %collective-permute-start.3) | collective-permute-done | bytes 163872 | tf_op jit(solution)/shard_map/ppermute | solution.py:317
  42.3 0.1 collective-permute-done.2.refs_1_
  42.4 0.4 collective-permute-start.6
  42.8 1.4 %meta.1.refs_11_ = bf16[16,128]{1,0:T(8,128)(2,1)} custom-call(s32[4,6]{1,0:T(4,128)} %index_ref.1, f32[4,6]{1,0:T(4,128)} %gate_ref.1, s32[4]{0:T(128)} %partner_ref.1), custom_call_target="tpu_custom_call" | custom-call | tf_op jit(solution)/shard_map/meta/pallas_call | solution.py:322
  44.3 0.7 copy-done.1
  44.9 7.8 %hidden.1 = (bf16[768,128]{1,0:T(8,128)(2,1)S(1)}, f32[8,128]{1,0:T(8,128)S(1)}, f32[8,128]{1,0:T(8,128)S(1)}, bf16[16,16,128]{2,1,0:T(8,128)(2,1)S(1)}) custom-call(bf16[16,5120]{1,0:T(8,128)(2,1)S(1)} %pad_maximum_fusion.2.refs_0_, bf16[16,5120]{1,0:T(8,128)(2,1)S(1)} %collective-permute-done.2.refs_1_, ...), custom_call_target="tpu_custom_call" | custom-call | tf_op jit(solution)/shard_map/hidden/pallas_call | solution.py:353
  52.8 13.4 %all_to_all.5.refs_8_ = bf16[16,16,128]{2,1,0:T(8,128)(2,1)S(1)} all-to-all(bf16[16,16,128]{2,1,0:T(8,128)(2,1)S(1)} %get-tuple-element.8), channel_id=1, replica_groups=mesh['dp'=2,'chip'=8,'core'=2] {'dp','chip'}, dimensions={0} | all-to-all | bytes 131072 | tf_op jit(solution)/shard_map/all_to_all | solution.py:372
  66.2 1.3 %collective-permute-done.10.refs_9_ = bf16[16,16,128]{2,1,0:T(8,128)(2,1)S(1)} collective-permute-done((bf16[16,16,128]{2,1,0:T(8,128)(2,1)S(1)}, bf16[16,16,128]{2,1,0:T(8,128)(2,1)S(1)}, u32[]{:S(2)}, u32[]{:S(2)}) %collective-permute-start.10) | collective-permute-done | bytes 65568 | tf_op jit(solution)/shard_map/ppermute | solution.py:317
  67.5 2.5 %gradient.1 = (f32[8,768]{1,0:T(8,128)}, f32[8,2560]{1,0:T(8,128)}) custom-call(bf16[16,5120]{1,0:T(8,128)(2,1)S(1)} %pad_maximum_fusion.2.refs_0_, bf16[16,5120]{1,0:T(8,128)(2,1)S(1)} %collective-permute-done.2.refs_1_, bf16[16,5120]{1,0:T(8,128)(2,1)S(1)} %collective-permute-done.3.refs_2_, bf16[16,5120]{1,0:T(8,128)(2,1)S(1)} %collective-permute-done.4.refs_3_, ...), custom_call_target="tpu_custom_call" | custom-call | tf_op jit(solution)/shard_map/gradient/pallas_call | solution.py:375
  (18 shorter events, 0.1 us)
Async XLA Ops:
  0.6 31.1 %copy-start.3 = (bf16[4,5120]{1,0:T(4,128)(2,1)S(1)}, bf16[4,5120]{1,0:T(4,128)(2,1)}, u32[]{:S(2)}) copy-start(bf16[4,5120]{1,0:T(4,128)(2,1)} %param.7) | copy-start | bytes 122884
  0.6 5.2 %collective-permute-start.9 = (bf16[8,2560]{1,0:T(8,128)(2,1)}, bf16[8,2560]{1,0:T(8,128)(2,1)S(1)}, u32[]{:S(2)}, u32[]{:S(2)}) collective-permute-start(bf16[8,2560]{1,0:T(8,128)(2,1)} %bitcast.7), channel_id=1, source_target_pairs={{0,16},{1,17},{2,18},{3,19},{4,20},{5,21},{6,22},{7,23},{8,24},{9,... | collective-permute-start | bytes 122888 | tf_op jit(solution)/shard_map/ppermute | solution.py:317
  5.8 0.6 copy-start.4
  7.9 4.7 %collective-permute-start.11 = (bf16[8,5120]{1,0:T(8,128)(2,1)}, bf16[8,5120]{1,0:T(8,128)(2,1)S(1)}, u32[]{:S(2)}, u32[]{:S(2)}) collective-permute-start(bf16[8,5120]{1,0:T(8,128)(2,1)} %whole_rows.1.refs_10_), channel_id=1, source_target_pairs={{0,4},{1,5},{2,6},{3,7},{4,0},{5,1},{6,2},{7,3},{8,12},{9,13},{10,... | collective-permute-start | bytes 245768 | tf_op jit(solution)/shard_map/ppermute | solution.py:317
  13.5 30.7 %copy-start = (bf16[8,5120]{1,0:T(8,128)(2,1)S(1)}, bf16[8,5120]{1,0:T(8,128)(2,1)}, u32[]{:S(2)}) copy-start(bf16[8,5120]{1,0:T(8,128)(2,1)} %whole_rows.1.refs_10_) | copy-start | bytes 245764
  13.5 30.7 %copy-start.2 = (bf16[1,8,768]{2,1,0:T(8,128)(2,1)S(1)}, bf16[1,8,768]{2,1,0:T(8,128)(2,1)}, u32[]{:S(2)}) copy-start(bf16[1,8,768]{2,1,0:T(8,128)(2,1)} %param.12) | copy-start | bytes 36868
  13.5 8.5 %collective-permute-start.12 = (bf16[16,5120]{1,0:T(8,128)(2,1)S(1)}, bf16[16,5120]{1,0:T(8,128)(2,1)S(1)}, u32[]{:S(2)}, u32[]{:S(2)}) collective-permute-start(bf16[16,5120]{1,0:T(8,128)(2,1)S(1)} %pad_maximum_fusion.3), channel_id=1, source_target_pairs={{0,8},{1,9},{2,10},{3,11},{4,12},{5,13},{6,14},{7,15},{8,0},{9,1},... | collective-permute-start | bytes 491528 | tf_op jit(solution)/shard_map/ppermute | solution.py:317
  16.6 8.0 %collective-permute-start = (bf16[4,5120]{1,0:T(4,128)(2,1)}, bf16[4,5120]{1,0:T(4,128)(2,1)S(1)}, u32[]{:S(2)}, u32[]{:S(2)}) collective-permute-start(bf16[4,5120]{1,0:T(4,128)(2,1)} %param.7), channel_id=1, source_target_pairs={{0,4},{1,5},{2,6},{3,7},{4,0},{5,1},{6,2},{7,3},{8,12},{9,13},{10,... | collective-permute-start | bytes 122888 | tf_op jit(solution)/shard_map/ppermute | solution.py:317
  23.0 7.1 %collective-permute-start.13 = (bf16[32,5120]{1,0:T(8,128)(2,1)S(1)}, bf16[32,5120]{1,0:T(8,128)(2,1)S(1)}, u32[]{:S(2)}, u32[]{:S(2)}) collective-permute-start(bf16[32,5120]{1,0:T(8,128)(2,1)S(1)} %pad_maximum_fusion.1), channel_id=1, source_target_pairs={{0,2},{1,3},{2,0},{3,1},{4,6},{5,7},{6,4},{7,5},{8,10},{9,11},{10,... | collective-permute-start | bytes 983048 | tf_op jit(solution)/shard_map/ppermute | solution.py:317
  25.4 6.3 %collective-permute-start.1 = (bf16[8,5120]{1,0:T(8,128)(2,1)S(1)}, bf16[8,5120]{1,0:T(8,128)(2,1)S(1)}, u32[]{:S(2)}, u32[]{:S(2)}) collective-permute-start(bf16[8,5120]{1,0:T(8,128)(2,1)S(1)} %pad_maximum_fusion.4), channel_id=1, source_target_pairs={{0,8},{1,9},{2,10},{3,11},{4,12},{5,13},{6,14},{7,15},{8,0},{9,1},... | collective-permute-start | bytes 245768 | tf_op jit(solution)/shard_map/ppermute | solution.py:317
  31.0 36.4 %collective-permute-start.14 = (bf16[64,5120]{1,0:T(8,128)(2,1)S(1)}, bf16[64,5120]{1,0:T(8,128)(2,1)S(1)}, u32[]{:S(2)}, u32[]{:S(2)}) collective-permute-start(bf16[64,5120]{1,0:T(8,128)(2,1)S(1)} %pad_maximum_fusion.refs_10_), channel_id=1, source_target_pairs={{0,1},{1,0},{2,3},{3,2},{4,5},{5,4},{6,7},{7,6},{8,9},{9,8},{10,11... | collective-permute-start | bytes 1966088 | tf_op jit(solution)/shard_map/ppermute | solution.py:317
  31.8 7.9 %collective-permute-start.4 = (bf16[16,5120]{1,0:T(8,128)(2,1)S(1)}, bf16[16,5120]{1,0:T(8,128)(2,1)S(1)}, u32[]{:S(2)}, u32[]{:S(2)}) collective-permute-start(bf16[16,5120]{1,0:T(8,128)(2,1)S(1)} %pad_maximum_fusion.2.refs_0_), channel_id=1, source_target_pairs={{0,18},{1,19},{2,16},{3,17},{4,22},{5,23},{6,20},{7,21},{8,26},{9,... | collective-permute-start | bytes 491528 | tf_op jit(solution)/shard_map/ppermute | solution.py:317
  33.8 8.5 %collective-permute-start.3 = (bf16[16,5120]{1,0:T(8,128)(2,1)S(1)}, bf16[16,5120]{1,0:T(8,128)(2,1)S(1)}, u32[]{:S(2)}, u32[]{:S(2)}) collective-permute-start(bf16[16,5120]{1,0:T(8,128)(2,1)S(1)} %pad_maximum_fusion.2.refs_0_), channel_id=1, source_target_pairs={{0,2},{1,3},{2,0},{3,1},{4,6},{5,7},{6,4},{7,5},{8,10},{9,11},{10,... | collective-permute-start | bytes 491528 | tf_op jit(solution)/shard_map/ppermute | solution.py:317
  34.8 7.6 %collective-permute-start.2 = (bf16[16,5120]{1,0:T(8,128)(2,1)S(1)}, bf16[16,5120]{1,0:T(8,128)(2,1)S(1)}, u32[]{:S(2)}, u32[]{:S(2)}) collective-permute-start(bf16[16,5120]{1,0:T(8,128)(2,1)S(1)} %pad_maximum_fusion.2.refs_0_), channel_id=1, source_target_pairs={{0,16},{1,17},{2,18},{3,19},{4,20},{5,21},{6,22},{7,23},{8,24},{9,... | collective-permute-start | bytes 491528 | tf_op jit(solution)/shard_map/ppermute | solution.py:317
  35.4 8.8 %collective-permute-start.5 = (bf16[16,5120]{1,0:T(8,128)(2,1)S(1)}, bf16[16,5120]{1,0:T(8,128)(2,1)S(1)}, u32[]{:S(2)}, u32[]{:S(2)}) collective-permute-start(bf16[16,5120]{1,0:T(8,128)(2,1)S(1)} %pad_maximum_fusion.2.refs_0_), channel_id=1, source_target_pairs={{0,1},{1,0},{2,3},{3,2},{4,5},{5,4},{6,7},{7,6},{8,9},{9,8},{10,11... | collective-permute-start | bytes 491528 | tf_op jit(solution)/shard_map/ppermute | solution.py:317
  39.7 4.5 %collective-permute-start.8 = (bf16[16,5120]{1,0:T(8,128)(2,1)S(1)}, bf16[16,5120]{1,0:T(8,128)(2,1)S(1)}, u32[]{:S(2)}, u32[]{:S(2)}) collective-permute-start(bf16[16,5120]{1,0:T(8,128)(2,1)S(1)} %collective-permute-done.4.refs_3_), channel_id=1, source_target_pairs={{0,1},{1,0},{2,3},{3,2},{4,5},{5,4},{6,7},{7,6},{8,9},{9,8},{10,11... | collective-permute-start | bytes 491528 | tf_op jit(solution)/shard_map/ppermute | solution.py:317
  42.3 1.9 %collective-permute-start.7 = (bf16[16,5120]{1,0:T(8,128)(2,1)S(1)}, bf16[16,5120]{1,0:T(8,128)(2,1)S(1)}, u32[]{:S(2)}, u32[]{:S(2)}) collective-permute-start(bf16[16,5120]{1,0:T(8,128)(2,1)S(1)} %collective-permute-done.3.refs_2_), channel_id=1, source_target_pairs={{0,1},{1,0},{2,3},{3,2},{4,5},{5,4},{6,7},{7,6},{8,9},{9,8},{10,11... | collective-permute-start | bytes 491528 | tf_op jit(solution)/shard_map/ppermute | solution.py:317
  42.4 1.8 %collective-permute-start.6 = (bf16[16,5120]{1,0:T(8,128)(2,1)S(1)}, bf16[16,5120]{1,0:T(8,128)(2,1)S(1)}, u32[]{:S(2)}, u32[]{:S(2)}) collective-permute-start(bf16[16,5120]{1,0:T(8,128)(2,1)S(1)} %collective-permute-done.2.refs_1_), channel_id=1, source_target_pairs={{0,1},{1,0},{2,3},{3,2},{4,5},{5,4},{6,7},{7,6},{8,9},{9,8},{10,11... | collective-permute-start | bytes 491528 | tf_op jit(solution)/shard_map/ppermute | solution.py:317
  44.3 0.7 copy-start.1
  66.2 1.3 %collective-permute-start.10 = (bf16[16,16,128]{2,1,0:T(8,128)(2,1)S(1)}, bf16[16,16,128]{2,1,0:T(8,128)(2,1)S(1)}, u32[]{:S(2)}, u32[]{:S(2)}) collective-permute-start(bf16[16,16,128]{2,1,0:T(8,128)(2,1)S(1)} %all_to_all.5.refs_8_), channel_id=1, source_target_pairs={{0,1},{1,0},{2,3},{3,2},{4,5},{5,4},{6,7},{7,6},{8,9},{9,8},{10,11... | collective-permute-start | bytes 196616 | tf_op jit(solution)/shard_map/ppermute | solution.py:317

commit v2 on v0

--- a/solution.py
+++ b/solution.py
@@ -1,13 +1,21 @@
+import functools
 import math
 
 import jax
 import jax.numpy as jnp
 from jax import lax
+from jax.experimental import pallas as pl
+from jax.experimental.pallas import tpu as pltpu
+from jax.sharding import Mesh
 from jax.sharding import PartitionSpec as P
 
 adapter_scale = 2.0
 control = 0.5
 highest_precision = lax.Precision.HIGHEST
+f32 = jnp.float32
+bf16 = jnp.bfloat16
+every = ("dp", "chip", "core")
+mib = 1 << 20
 
 
 def route_tables(chosen_expert_index, router_gate_weight, experts, capacity):
@@ -33,7 +41,7 @@
     return (jax.nn.silu(both[0]) * both[1]).astype(jnp.bfloat16)
 
 
-def body(
+def slot_body(
     tokens,
     chosen_expert_index,
     router_gate_weight,
@@ -107,20 +115,368 @@
     return (down_factor_gradient[None], up_factor_gradient[None])
 
 
+def mask_of(block):
+    return (
+        ((block & 1) << 3)
+        | (((block >> 1) & 1) << 2)
+        | (((block >> 2) & 1) << 4)
+        | (((block >> 3) & 1) << 1)
+        | ((block >> 4) & 1)
+    )
+
+
+def own_number():
+    return (lax.axis_index("dp") * lax.axis_size("chip") + lax.axis_index("chip")) * 2 + (
+        lax.axis_index("core")
+    )
+
+
+def dot(left, right, left_dim, right_dim, precision=None):
+    return lax.dot_general(
+        left,
+        right,
+        (((left_dim,), (right_dim,)), ((), ())),
+        precision=precision,
+        preferred_element_type=f32,
+    )
+
+
+def split_two(value):
+    high = value.astype(bf16)
+    return high, (value - high.astype(f32)).astype(bf16)
+
+
+def order_table(count):
+    lane = lax.broadcasted_iota(jnp.int32, (count, count), 1)
+    row = lax.broadcasted_iota(jnp.int32, (count, count), 0)
+    whole = ((mask_of(lane >> 2) ^ own_number()) << 2) | (lane & 3)
+    return (row == whole).astype(f32).astype(bf16)
+
+
+def start_kernel(
+    x_ref, u_ref, index_ref, gate_ref, partner_ref, out_ref, up_ref, index_v, gate_v, partner_s, sems
+):
+    count, width = x_ref.shape
+    copies = [
+        pltpu.make_async_copy(index_ref, index_v, sems.at[0]),
+        pltpu.make_async_copy(gate_ref, gate_v, sems.at[1]),
+        pltpu.make_async_copy(partner_ref, partner_s, sems.at[2]),
+        pltpu.make_async_copy(u_ref, up_ref, sems.at[3]),
+        pltpu.make_async_copy(x_ref, out_ref.at[:, pl.ds(0, width)], sems.at[4]),
+    ]
+    for copy in copies:
+        copy.start()
+    for copy in copies[:3]:
+        copy.wait()
+    lane = lax.broadcasted_iota(jnp.int32, (count, 128), 1)
+    row = lax.broadcasted_iota(jnp.int32, (count, 128), 0)
+    index, gate = index_v[...], gate_v[...]
+    dense = jnp.zeros((count, 128), f32)
+    for k in range(index.shape[1]):
+        dense = dense + jnp.where((lane & 15) == index[:, k : k + 1], gate[:, k : k + 1], 0.0)
+    mates = jnp.zeros((count, 128), f32)
+    for t in range(count):
+        mates = mates + jnp.where((row == t) & (lane == 48), partner_s[t].astype(f32), 0.0)
+    high = dense.astype(bf16).astype(f32)
+    middle = (dense - high).astype(bf16).astype(f32)
+    low = dense - high - middle
+    parts = jnp.where(lane < 16, high, jnp.where(lane < 32, middle, jnp.where(lane < 48, low, mates)))
+    out_ref[:, pl.ds(width, 128)] = parts.astype(bf16)
+    copies[3].wait()
+    copies[4].wait()
+
+
+def fetch_kernel(first, w_ref, v_ref, w_out, v_out, sems):
+    units = w_out.shape[1]
+    parts = sems.shape[0] - 1
+    rows = units // parts
+    copies = [pltpu.make_async_copy(v_ref.at[:, pl.ds(first, units)], v_out, sems.at[parts])]
+    for i in range(parts):
+        copies.append(
+            pltpu.make_async_copy(
+                w_ref.at[:, pl.ds(first + i * rows, rows), :], w_out.at[:, pl.ds(i * rows, rows), :], sems.at[i]
+            )
+        )
+    for copy in copies:
+        copy.start()
+    for copy in copies:
+        copy.wait()
+
+
+def join_kernel(first_ref, second_ref, out_ref):
+    rows = first_ref.shape[0]
+    out_ref[pl.ds(0, rows), :] = first_ref[...]
+    out_ref[pl.ds(rows, rows), :] = second_ref[...]
+
+
+def hidden_kernel(step, pieces, *refs):
+    x_refs = refs[:pieces]
+    early_w, early_v, late_w, late_v, own_up, other_up = refs[pieces : pieces + 6]
+    hid_ref, low_ref, cross_ref, gate_ref, x_all = refs[pieces + 6 :]
+    at = 0
+    for ref in x_refs:
+        x_all[pl.ds(at, ref.shape[0]), :] = ref[...]
+        at += ref.shape[0]
+    width = early_w.shape[2]
+    half = width // 2
+    x = x_all[:, pl.ds(0, width)]
+    low = jnp.zeros(low_ref.shape, f32)
+    base = 0
+    for w_ref, v_ref in ((early_w, early_v), (late_w, late_v)):
+        for at in range(0, w_ref.shape[1], step):
+            gate = dot(w_ref[0, pl.ds(at, step), :], x, 1, 1)
+            up = dot(w_ref[1, pl.ds(at, step), :], x, 1, 1)
+            hidden = (gate / (1.0 + jnp.exp(-gate)) * up).astype(bf16)
+            hid_ref[pl.ds(base + at, step), :] = hidden
+            low = low + dot(v_ref[:, pl.ds(at, step)], hidden, 1, 0)
+        base += w_ref.shape[1]
+
+    dp = lax.axis_index("dp")
+    here = pl.ds(pl.multiple_of(dp * half, 128), half)
+    there = pl.ds(pl.multiple_of((1 - dp) * half, 128), half)
+    cross_ref[...] = dot(own_up[...], x_all[:, here], 1, 1) + dot(other_up[...], x_all[:, there], 1, 1)
+    lane = lax.broadcasted_iota(jnp.int32, (16, 128), 1)
+    row = lax.broadcasted_iota(jnp.int32, (16, 128), 0)
+    mine = ((lane & 15) == (own_number() & 15)) & (lane < 48)
+    pick = jnp.where(row < 8, mine.astype(f32), (lane == 48).astype(f32)).astype(bf16)
+    gates = dot(pick, x_all[:, pl.ds(width, 128)], 1, 1)
+    gate_ref[...] = gates
+    low_ref[...] = low * gates[0:8]
+
+
+def send_kernel(low_ref, up_near, sibling_ref, gram_ref, send_ref):
+    count = low_ref.shape[1]
+    gram_ref[...] = dot(up_near[0:8, :], up_near[...], 1, 1)
+    other = dot(sibling_ref[...], up_near[...], 1, 1)
+    ordered = dot(low_ref[...].astype(bf16), order_table(count), 1, 1)
+    products = jnp.concatenate([gram_ref[...], other], axis=1)
+    block = jnp.concatenate([ordered, products], axis=0).astype(bf16)
+    for i in range(send_ref.shape[0]):
+        send_ref[i] = block
+
+
+def gradient_kernel(
+    near_ref,
+    far_ref,
+    up_near,
+    up_far,
+    x_all,
+    hid_ref,
+    low_ref,
+    gram_ref,
+    cross_ref,
+    gate_ref,
+    down_out,
+    up_out,
+    blocks_buf,
+):
+    tokens = hid_ref.shape[1]
+    blocks = tokens // 4
+    half = up_out.shape[1]
+    dp = lax.axis_index("dp")
+    chip = lax.axis_index("chip")
+    chips = lax.axis_size("chip")
+    for b in range(blocks):
+        away = ((b & 1) << 0) | (((b >> 1) & 1) << 2) | (((b >> 2) & 1) << 1)
+        source = far_ref if (b >> 3) & 1 else near_ref
+        blocks_buf[b] = source[(dp ^ (b >> 4)) * chips + (chip ^ away)]
+    local = dot(blocks_buf[...].reshape(blocks * 16, tokens), order_table(tokens), 1, 0)
+    local = local.reshape(2, 16, 16, tokens)[:, :, 0:8]
+    lows = (local[0] + local[1]).reshape(tokens, tokens)
+    own_low = low_ref[...] + local[1, 0]
+    ends = [blocks_buf[b].astype(f32)[8:16] for b in (16, 8, 24)]
+    near_rows = up_near.shape[0]
+    gram = jnp.concatenate(
+        [gram_ref[...] + ends[0][:, :near_rows], ends[1][:, near_rows:] + ends[2][:, near_rows:]], axis=1
+    )
+
+    gates = gate_ref[...]
+    lane = lax.broadcasted_iota(jnp.int32, (tokens, tokens), 1)
+    row = lax.broadcasted_iota(jnp.int32, (tokens, tokens), 0)
+    mate = (lane & ~3) | gates[8:9].astype(jnp.int32)
+    apart = (row == lane).astype(f32) - (row == mate).astype(f32)
+    factors = jnp.concatenate([adapter_scale * lows, -control * apart], axis=0)
+    scale = 2.0 / math.sqrt(tokens)
+
+    mixed = dot(own_low, factors, 1, 1, highest_precision)
+    high, low = split_two((adapter_scale * scale) * mixed)
+    both = jnp.concatenate([high, low], axis=0)
+    here = pl.ds(pl.multiple_of(dp * half, 128), half)
+    up = (
+        dot(both[:, :near_rows], up_near[...], 1, 0)
+        + dot(both[:, near_rows:tokens], up_far[...], 1, 0)
+        + dot(both[:, tokens:], x_all[:, here], 1, 0)
+    )
+    up_out[...] = up[0:8] + up[8:16]
+
+    products = jnp.concatenate([gram, cross_ref[...]], axis=1)
+    cot_low = dot(products, factors, 1, 0, highest_precision) * gates[0:8]
+    high, low = split_two((adapter_scale * scale) * cot_low)
+    both = jnp.concatenate([high, low], axis=0)
+    down = dot(both, hid_ref[...], 1, 1)
+    down_out[...] = down[0:8] + down[8:16]
+
+
+def dense_body(
+    tokens,
+    chosen_expert_index,
+    router_gate_weight,
+    partner,
+    gate_up_weight,
+    adapter_down_weight,
+    adapter_up_weight,
+):
+    tok_count, width = tokens.shape
+    devices = lax.axis_size("dp") * lax.axis_size("chip") * lax.axis_size("core")
+    total = tok_count * devices
+    units = gate_up_weight.shape[2]
+    rank = adapter_up_weight.shape[1]
+    half = adapter_up_weight.shape[2]
+    vmem = pl.BlockSpec(memory_space=pltpu.VMEM)
+    hbm = pl.BlockSpec(memory_space=pltpu.HBM)
+
+    def swap(value, mask):
+        return lax.ppermute(value, every, [(i, i ^ mask) for i in range(devices)])
+
+    def grow(value, mask):
+        return jnp.concatenate([value, swap(value, mask)], axis=0)
+
+    def stay(value):
+        return pltpu.with_memory_space_constraint(value, pltpu.HBM)
+
+    def after(values, other):
+        return lax.optimization_barrier((values, other))[0]
+
+    def after(value, other):
+        return lax.optimization_barrier((value, other))[0]
+
+    column, own_up = pl.pallas_call(
+        start_kernel,
+        out_shape=(
+            pltpu.VMEM((tok_count, width + 128), bf16),
+            pltpu.VMEM((rank, half), bf16),
+        ),
+        in_specs=[hbm] * 5,
+        out_specs=(vmem,) * 2,
+        scratch_shapes=[
+            pltpu.VMEM(chosen_expert_index.shape, jnp.int32),
+            pltpu.VMEM(router_gate_weight.shape, f32),
+            pltpu.SMEM(partner.shape, jnp.int32),
+            pltpu.SemaphoreType.DMA((5,)),
+        ],
+        compiler_params=pltpu.CompilerParams(vmem_limit_bytes=2 * mib),
+        name="start",
+    )(*map(stay, (tokens, adapter_up_weight[0], chosen_expert_index, router_gate_weight, partner)))
+
+    def fetch(first, name, order):
+        w, v = after((gate_up_weight[0], adapter_down_weight[0]), order)
+        return pl.pallas_call(
+            functools.partial(fetch_kernel, first),
+            out_shape=(pltpu.VMEM((2, units // 2, width), bf16), pltpu.VMEM((rank, units // 2), bf16)),
+            in_specs=[hbm, hbm],
+            out_specs=(vmem, vmem),
+            scratch_shapes=[pltpu.SemaphoreType.DMA((4,))],
+            compiler_params=pltpu.CompilerParams(vmem_limit_bytes=2 * mib),
+            cost_estimate=pl.CostEstimate(flops=0, bytes_accessed=8 * mib, transcendentals=0),
+            name=name,
+        )(stay(w), stay(v))
+
+    weights = fetch(0, "fetch_early", column)
+    first = grow(column, 8)
+    other_up, sibling, ups = swap(own_up, 16), swap(own_up, 1), swap(own_up, 2)
+    first, weights, other_up, sibling, ups = lax.optimization_barrier((first, weights, other_up, sibling, ups))
+    late_weights = fetch(units // 2, "fetch_late", first)
+    column = grow(first, 4)
+    column, late_weights = lax.optimization_barrier((column, late_weights))
+    ups = jnp.concatenate([own_up, ups], axis=0)
+    third = swap(ups, 8)
+    near = [swap(column, 16), swap(column, 2), swap(column, 18)]
+    ups = pl.pallas_call(
+        join_kernel,
+        out_shape=pltpu.VMEM((4 * rank, half), bf16),
+        in_specs=[vmem, vmem],
+        out_specs=vmem,
+        compiler_params=pltpu.CompilerParams(vmem_limit_bytes=2 * mib),
+        cost_estimate=pl.CostEstimate(flops=0, bytes_accessed=8 * mib, transcendentals=0),
+        name="join",
+    )(*after((ups, third), column))
+    fourth = swap(ups, 4)
+    near = [column] + near
+    pieces = near + [swap(piece, 1) for piece in near]
+
+    count = len(pieces)
+    hidden, low, cross, gates, everything = pl.pallas_call(
+        functools.partial(hidden_kernel, units // 4, count),
+        out_shape=(
+            pltpu.VMEM((units, total), bf16),
+            pltpu.VMEM((rank, total), f32),
+            pltpu.VMEM((rank, total), f32),
+            pltpu.VMEM((16, total), f32),
+            pltpu.VMEM((total, width + 128), bf16),
+        ),
+        in_specs=[vmem] * (count + 6),
+        out_specs=(vmem,) * 5,
+        compiler_params=pltpu.CompilerParams(vmem_limit_bytes=8 * mib),
+        cost_estimate=pl.CostEstimate(flops=0, bytes_accessed=16 * mib, transcendentals=0),
+        name="hidden",
+    )(*pieces, *weights, *late_weights, own_up, other_up)
+
+    up_near = jnp.concatenate(after((ups, fourth), low), axis=0)
+    up_far = swap(up_near, 1)
+    gram, send = pl.pallas_call(
+        send_kernel,
+        out_shape=(
+            jax.ShapeDtypeStruct((rank, total // 2), f32),
+            jax.ShapeDtypeStruct((devices // 2, 16, total), bf16),
+        ),
+        in_specs=[vmem] * 3,
+        out_specs=(vmem,) * 2,
+        compiler_params=pltpu.CompilerParams(vmem_limit_bytes=4 * mib),
+        name="send",
+    )(low, up_near, sibling)
+
+    from_near = lax.all_to_all(send, ("dp", "chip"), split_axis=0, concat_axis=0, tiled=True)
+    from_far = swap(from_near, 1)
+
+    down, up = pl.pallas_call(
+        gradient_kernel,
+        out_shape=(
+            jax.ShapeDtypeStruct((rank, units), f32),
+            jax.ShapeDtypeStruct((rank, half), f32),
+        ),
+        in_specs=[vmem] * 10,
+        out_specs=(vmem, vmem),
+        scratch_shapes=[pltpu.VMEM((devices, 16, total), bf16)],
+        compiler_params=pltpu.CompilerParams(vmem_limit_bytes=16 * mib),
+        name="gradient",
+    )(
+        from_near, from_far, up_near, up_far, everything, hidden, low, gram, cross, gates
+    )
+    return (down[None], up[None])
+
+
 def solution(mesh):
+    groups, experts = mesh.shape["dp"], mesh.shape["expert"]
+    if (groups, experts) == (2, 16):
+        cut = Mesh(mesh.devices.reshape(groups, experts // 2, 2), every)
+        data, owners = every, ("chip", "core")
+        run, mesh = dense_body, cut
+    else:
+        data, owners = ("dp", "expert"), "expert"
+        run = slot_body
     placed = (
-        P(("dp", "expert"), None),
-        P(("dp", "expert"), None),
-        P(("dp", "expert"), None),
-        P(("dp", "expert")),
-        P("expert", None, "dp", None),
-        P("expert", None, "dp"),
-        P("expert", None, "dp"),
+        P(data, None),
+        P(data, None),
+        P(data, None),
+        P(data),
+        P(owners, None, "dp", None),
+        P(owners, None, "dp"),
+        P(owners, None, "dp"),
     )
     return jax.shard_map(
-        body,
+        run,
         mesh=mesh,
         in_specs=placed,
-        out_specs=(P("expert", None, "dp"), P("expert", None, "dp")),
+        out_specs=(P(owners, None, "dp"), P(owners, None, "dp")),
         check_vma=False,
     )

time: 133 us -> 48.2 us (0.36)
  blocking collectives: 87.5 us -> 10.4 us
  matrix products: 16.9 us -> 0 us
  Pallas kernels: 0 us -> 14.6 us
  starting transfers between devices: 3.59 us -> 14.2 us
  waiting for transfers between devices: 15.7 us -> 7.93 us
  local copies, waits for them, and re-layouts: 7.42 us -> 0.03 us
    all_to_all x4 -> x1, blocking collectives: 63.5 us -> 10.4 us  [dense_body(): lax.all_to_all(send, ('dp', 'chip'), split_axis=0, concat_axis=0, tiled=T...]
    dot_general x11 -> x0, matrix products: 16.9 us -> none  [the longest x1 10.4 us: expert_hidden(): jnp.einsum('gfd,nd->gfn', w_local, flat_rows, preferred_element_type=jnp....]
    all_to_all x1 -> x0, waiting for transfers between devices: 15.7 us -> none  [body(): lax.all_to_all(lax.all_to_all(change_rows, 'dp', split_axis=0, concat_axi...]
    pallas_call x0 -> x7, Pallas kernels: none -> 14.6 us  [the longest x2 6.72 us: fetch(): pl.pallas_call(functools.partial(fetch_kernel, first), out_shape=(pltpu.V...]
    ppermute x0 -> x16, starting transfers between devices: none -> 14.2 us  [swap(): return lax.ppermute(value, every, [(i, i ^ mask) for i in range(devices)])]
    all_gather x1 -> x0, blocking collectives: 14.1 us -> none  [body(): lax.all_gather(arrived, 'dp', axis=0, tiled=True)]
    psum x2 -> x0, blocking collectives: 9.88 us -> none  [the longest x1 4.95 us: body(): cotangent_narrow = lax.psum(partial_cot, 'dp')]
    ppermute x0 -> x16, waiting for transfers between devices: none -> 7.93 us  [swap(): return lax.ppermute(value, every, [(i, i ^ mask) for i in range(devices)])]
  transfers between devices with their start and end apart: 1 -> 16, of which waited for: 1 -> 6; matrix products, arithmetic and copies ran while one was open for 1% -> 0% of each run, Pallas kernels for 0% -> 24%
where the time goes in v2:
time: 48.2 us; the launch traced here: 48 us
  Pallas kernels  14.6 us (30%)
  starting transfers between devices  14.2 us (29%)
  blocking collectives  10.4 us (22%)
  waiting for transfers between devices  7.93 us (16%)
  between operations  0.74 us (2%)
    ppermute x16, starting transfers between devices, swap(): return lax.ppermute(value, every, [(i, i ^ mask) for i in range(devices)])  14.2 us
    all_to_all x1, blocking collectives, dense_body(): lax.all_to_all(send, ('dp', 'chip'), split_axis=0, concat_axis=0, tiled=T...  10.4 us
    ppermute x16, waiting for transfers between devices, swap(): return lax.ppermute(value, every, [(i, i ^ mask) for i in range(devices)])  7.93 us
    pallas_call x2, Pallas kernels, fetch(): pl.pallas_call(functools.partial(fetch_kernel, first), out_shape=(pltpu.V...  6.72 us
    pallas_call x1, Pallas kernels, dense_body(): pl.pallas_call(functools.partial(hidden_kernel, units // 4, count), out_s...  4.92 us
    pallas_call x1, Pallas kernels, dense_body(): pl.pallas_call(gradient_kernel, out_shape=(jax.ShapeDtypeStruct((rank, un...  1.67 us
  transfers between devices with their start and end apart: 16, of which 6 were waited for; matrix products, arithmetic and copies ran while one was open for 0% of the time, Pallas kernels for 24%

profile of v2, /device:TPU:0, one launch (start us, length us, event | category | flops | bytes accessed | tf_op | source)
XLA Modules:
  0.0 48.0 jit_solution(528416131334763820)
XLA Ops:
  0.6 0.9 %start.1 = (bf16[4,5248]{1,0:T(4,128)(2,1)S(1)}, bf16[8,2560]{1,0:T(8,128)(2,1)S(1)}) custom-call(bf16[4,5120]{1,0:T(4,128)(2,1)} %x_ref.1, bf16[8,2560]{1,0:T(8,128)(2,1)} %bitcast.9, s32[4,6]{1,0:T(4,128)} %index_ref.1, f32[4,6]{1,0:T(4,128)} %gate_ref.1, s32[4]{0:T(128)} %partner_ref.1), custom_call_target="tpu_custom_call" | custom-call | tf_op jit(solution)/shard_map/start/pallas_call | solution.py:353
  1.6 4.1 %collective-permute-start = (bf16[4,5248]{1,0:T(4,128)(2,1)S(1)}, bf16[4,5248]{1,0:T(4,128)(2,1)S(1)}, u32[]{:S(2)}, u32[]{:S(2)}) collective-permute-start(bf16[4,5248]{1,0:T(4,128)(2,1)S(1)} %get-tuple-element.34), channel_id=1, source_target_pairs={{0,8},{1,9},{2,10},{3,11},{4,12},{5,13},{6,14},{7,15},{8,0},{9,1},... | collective-permute-start | bytes 125960 | tf_op jit(solution)/shard_map/ppermute | solution.py:339
  5.7 1.5 %collective-permute-start.1 = (bf16[8,2560]{1,0:T(8,128)(2,1)S(1)}, bf16[8,2560]{1,0:T(8,128)(2,1)S(1)}, u32[]{:S(2)}, u32[]{:S(2)}) collective-permute-start(bf16[8,2560]{1,0:T(8,128)(2,1)S(1)} %get-tuple-element.39.refs_12_), channel_id=1, source_target_pairs={{0,16},{1,17},{2,18},{3,19},{4,20},{5,21},{6,22},{7,23},{8,24},{9,... | collective-permute-start | bytes 122888 | tf_op jit(solution)/shard_map/ppermute | solution.py:339
  7.2 0.0 collective-permute-start.2
  7.2 1.5 %collective-permute-start.3 = (bf16[8,2560]{1,0:T(8,128)(2,1)S(1)}, bf16[8,2560]{1,0:T(8,128)(2,1)S(1)}, u32[]{:S(2)}, u32[]{:S(2)}) collective-permute-start(bf16[8,2560]{1,0:T(8,128)(2,1)S(1)} %get-tuple-element.39.refs_12_), channel_id=1, source_target_pairs={{0,2},{1,3},{2,0},{3,1},{4,6},{5,7},{6,4},{7,5},{8,10},{9,11},{10,... | collective-permute-start | bytes 122888 | tf_op jit(solution)/shard_map/ppermute | solution.py:339
  8.7 3.4 %fetch_early.1 = (bf16[2,384,5120]{2,1,0:T(8,128)(2,1)S(1)}, bf16[8,384]{1,0:T(8,128)(2,1)S(1)}) custom-call(bf16[2,768,5120]{2,1,0:T(8,128)(2,1)} %bitcast.5, bf16[8,768]{1,0:T(8,128)(2,1)} %bitcast.7), custom_call_target="tpu_custom_call" | custom-call | bytes 8388608 | tf_op jit(solution)/shard_map/fetch_early/pallas_call | solution.py:373
  12.1 0.0 collective-permute-done
  12.1 0.0 collective-permute-done.1.refs_13_
  12.2 1.6 %collective-permute-start.4 = (bf16[8,5248]{1,0:T(8,128)(2,1)S(1)}, bf16[8,5248]{1,0:T(8,128)(2,1)S(1)}, u32[]{:S(2)}, u32[]{:S(2)}) collective-permute-start(bf16[8,5248]{1,0:T(8,128)(2,1)S(1)} %pad_maximum_fusion.1), channel_id=1, source_target_pairs={{0,4},{1,5},{2,6},{3,7},{4,0},{5,1},{6,2},{7,3},{8,12},{9,13},{10,... | collective-permute-start | bytes 251912 | tf_op jit(solution)/shard_map/ppermute | solution.py:339
  13.8 3.4 %fetch_late.1 = (bf16[2,384,5120]{2,1,0:T(8,128)(2,1)S(1)}, bf16[8,384]{1,0:T(8,128)(2,1)S(1)}) custom-call(bf16[2,768,5120]{2,1,0:T(8,128)(2,1)} %bitcast.6, bf16[8,768]{1,0:T(8,128)(2,1)} %bitcast.8), custom_call_target="tpu_custom_call" | custom-call | bytes 8388608 | tf_op jit(solution)/shard_map/fetch_late/pallas_call | solution.py:373
  17.2 0.0 collective-permute-done.4
  17.2 0.6 %collective-permute-start.5 = (bf16[16,5248]{1,0:T(8,128)(2,1)S(1)}, bf16[16,5248]{1,0:T(8,128)(2,1)S(1)}, u32[]{:S(2)}, u32[]{:S(2)}) collective-permute-start(bf16[16,5248]{1,0:T(8,128)(2,1)S(1)} %pad_maximum_fusion.refs_0_), channel_id=1, source_target_pairs={{0,16},{1,17},{2,18},{3,19},{4,20},{5,21},{6,22},{7,23},{8,24},{9,... | collective-permute-start | bytes 503816 | tf_op jit(solution)/shard_map/ppermute | solution.py:339
  17.8 0.5 %collective-permute-start.6 = (bf16[16,5248]{1,0:T(8,128)(2,1)S(1)}, bf16[16,5248]{1,0:T(8,128)(2,1)S(1)}, u32[]{:S(2)}, u32[]{:S(2)}) collective-permute-start(bf16[16,5248]{1,0:T(8,128)(2,1)S(1)} %pad_maximum_fusion.refs_0_), channel_id=1, source_target_pairs={{0,2},{1,3},{2,0},{3,1},{4,6},{5,7},{6,4},{7,5},{8,10},{9,11},{10,... | collective-permute-start | bytes 503816 | tf_op jit(solution)/shard_map/ppermute | solution.py:339
  18.3 2.4 %collective-permute-start.7 = (bf16[16,5248]{1,0:T(8,128)(2,1)S(1)}, bf16[16,5248]{1,0:T(8,128)(2,1)S(1)}, u32[]{:S(2)}, u32[]{:S(2)}) collective-permute-start(bf16[16,5248]{1,0:T(8,128)(2,1)S(1)} %pad_maximum_fusion.refs_0_), channel_id=1, source_target_pairs={{0,18},{1,19},{2,16},{3,17},{4,22},{5,23},{6,20},{7,21},{8,26},{9,... | collective-permute-start | bytes 503816 | tf_op jit(solution)/shard_map/ppermute | solution.py:339
  20.8 0.3 collective-permute-start.12
  21.1 0.0 collective-permute-start.8
  21.1 3.3 %collective-permute-done.5.refs_1_ = bf16[16,5248]{1,0:T(8,128)(2,1)S(1)} collective-permute-done((bf16[16,5248]{1,0:T(8,128)(2,1)S(1)}, bf16[16,5248]{1,0:T(8,128)(2,1)S(1)}, u32[]{:S(2)}, u32[]{:S(2)}) %collective-permute-start.5) | collective-permute-done | bytes 167968 | tf_op jit(solution)/shard_map/ppermute | solution.py:339
  24.4 2.8 %collective-permute-done.6.refs_2_ = bf16[16,5248]{1,0:T(8,128)(2,1)S(1)} collective-permute-done((bf16[16,5248]{1,0:T(8,128)(2,1)S(1)}, bf16[16,5248]{1,0:T(8,128)(2,1)S(1)}, u32[]{:S(2)}, u32[]{:S(2)}) %collective-permute-start.6) | collective-permute-done | bytes 167968 | tf_op jit(solution)/shard_map/ppermute | solution.py:339
  27.3 0.5 %collective-permute-start.11 = (bf16[16,5248]{1,0:T(8,128)(2,1)S(1)}, bf16[16,5248]{1,0:T(8,128)(2,1)S(1)}, u32[]{:S(2)}, u32[]{:S(2)}) collective-permute-start(bf16[16,5248]{1,0:T(8,128)(2,1)S(1)} %collective-permute-done.7.refs_3_), channel_id=1, source_target_pairs={{0,1},{1,0},{2,3},{3,2},{4,5},{5,4},{6,7},{7,6},{8,9},{9,8},{10,11... | collective-permute-start | bytes 503816 | tf_op jit(solution)/shard_map/ppermute | solution.py:339
  27.8 0.8 %collective-permute-start.13 = (bf16[32,2560]{1,0:T(8,128)(2,1)S(1)}, bf16[32,2560]{1,0:T(8,128)(2,1)S(1)}, u32[]{:S(2)}, u32[]{:S(2)}) collective-permute-start(bf16[32,2560]{1,0:T(8,128)(2,1)S(1)} %join.1), channel_id=1, source_target_pairs={{0,4},{1,5},{2,6},{3,7},{4,0},{5,1},{6,2},{7,3},{8,12},{9,13},{10,... | collective-permute-start | bytes 491528 | tf_op jit(solution)/shard_map/ppermute | solution.py:339
  28.6 0.0 collective-permute-done.9.refs_5_
  28.6 0.1 collective-permute-done.10.refs_6_
  28.7 0.2 collective-permute-done.11.refs_7_
  28.9 4.9 %hidden.1 = (bf16[768,128]{1,0:T(8,128)(2,1)S(1)}, f32[8,128]{1,0:T(8,128)S(1)}, f32[8,128]{1,0:T(8,128)S(1)}, f32[16,128]{1,0:T(8,128)S(1)}, bf16[128,5248]{1,0:T(8,128)(2,1)S(1)}) custom-call(bf16[16,5248]{1,0:T(8,128)(2,1)S(1)} %pad_maximum_fusion.refs_0_, bf16[16,5248]{1,0:T(8,128)(2,1)S(1)} %collective-permute-done.5.refs_1_, ...), custom_call_target="tpu_custom_call" | custom-call | bytes 16777216 | tf_op jit(solution)/shard_map/hidden/pallas_call | solution.py:408
  33.8 0.2 collective-permute-done.13
  34.0 0.3 collective-permute-start.15
  34.3 0.4 send.1
  34.6 10.4 %all_to_all.5.near_ref = bf16[16,16,128]{2,1,0:T(8,128)(2,1)S(1)} all-to-all(bf16[16,16,128]{2,1,0:T(8,128)(2,1)S(1)} %get-tuple-element.58), channel_id=1, replica_groups=mesh['dp'=2,'chip'=8,'core'=2] {'dp','chip'}, dimensions={0} | all-to-all | bytes 131072 | tf_op jit(solution)/shard_map/all_to_all | solution.py:438
  45.0 0.0 collective-permute-start.14
  45.0 1.3 %collective-permute-done.14.far_ref = bf16[16,16,128]{2,1,0:T(8,128)(2,1)S(1)} collective-permute-done((bf16[16,16,128]{2,1,0:T(8,128)(2,1)S(1)}, bf16[16,16,128]{2,1,0:T(8,128)(2,1)S(1)}, u32[]{:S(2)}, u32[]{:S(2)}) %collective-permute-start.14) | collective-permute-done | bytes 65568 | tf_op jit(solution)/shard_map/ppermute | solution.py:339
  46.3 0.0 collective-permute-done.15.up_far
  46.3 1.7 %gradient.1 = (f32[8,768]{1,0:T(8,128)}, f32[8,2560]{1,0:T(8,128)}) custom-call(bf16[16,16,128]{2,1,0:T(8,128)(2,1)S(1)} %all_to_all.5.near_ref, bf16[16,16,128]{2,1,0:T(8,128)(2,1)S(1)} %collective-permute-done.14.far_ref, bf16[64,2560]{1,0:T(8,128)(2,1)S(1)} %constant_dynamic-update-slice_fusion.2.up_near, ...), custom_call_target="tpu_custom_call" | custom-call | tf_op jit(solution)/shard_map/gradient/pallas_call | solution.py:441
  (14 shorter events, 0.1 us)
Async XLA Ops:
  1.6 10.5 %collective-permute-start = (bf16[4,5248]{1,0:T(4,128)(2,1)S(1)}, bf16[4,5248]{1,0:T(4,128)(2,1)S(1)}, u32[]{:S(2)}, u32[]{:S(2)}) collective-permute-start(bf16[4,5248]{1,0:T(4,128)(2,1)S(1)} %get-tuple-element.34), channel_id=1, source_target_pairs={{0,8},{1,9},{2,10},{3,11},{4,12},{5,13},{6,14},{7,15},{8,0},{9,1},... | collective-permute-start | bytes 125960 | tf_op jit(solution)/shard_map/ppermute | solution.py:339
  5.7 6.5 %collective-permute-start.1 = (bf16[8,2560]{1,0:T(8,128)(2,1)S(1)}, bf16[8,2560]{1,0:T(8,128)(2,1)S(1)}, u32[]{:S(2)}, u32[]{:S(2)}) collective-permute-start(bf16[8,2560]{1,0:T(8,128)(2,1)S(1)} %get-tuple-element.39.refs_12_), channel_id=1, source_target_pairs={{0,16},{1,17},{2,18},{3,19},{4,20},{5,21},{6,22},{7,23},{8,24},{9,... | collective-permute-start | bytes 122888 | tf_op jit(solution)/shard_map/ppermute | solution.py:339
  7.2 5.0 %collective-permute-start.2 = (bf16[8,2560]{1,0:T(8,128)(2,1)S(1)}, bf16[8,2560]{1,0:T(8,128)(2,1)S(1)}, u32[]{:S(2)}, u32[]{:S(2)}) collective-permute-start(bf16[8,2560]{1,0:T(8,128)(2,1)S(1)} %get-tuple-element.39.refs_12_), channel_id=1, source_target_pairs={{0,1},{1,0},{2,3},{3,2},{4,5},{5,4},{6,7},{7,6},{8,9},{9,8},{10,11... | collective-permute-start | bytes 122888 | tf_op jit(solution)/shard_map/ppermute | solution.py:339
  7.2 5.0 %collective-permute-start.3 = (bf16[8,2560]{1,0:T(8,128)(2,1)S(1)}, bf16[8,2560]{1,0:T(8,128)(2,1)S(1)}, u32[]{:S(2)}, u32[]{:S(2)}) collective-permute-start(bf16[8,2560]{1,0:T(8,128)(2,1)S(1)} %get-tuple-element.39.refs_12_), channel_id=1, source_target_pairs={{0,2},{1,3},{2,0},{3,1},{4,6},{5,7},{6,4},{7,5},{8,10},{9,11},{10,... | collective-permute-start | bytes 122888 | tf_op jit(solution)/shard_map/ppermute | solution.py:339
  12.2 5.0 %collective-permute-start.4 = (bf16[8,5248]{1,0:T(8,128)(2,1)S(1)}, bf16[8,5248]{1,0:T(8,128)(2,1)S(1)}, u32[]{:S(2)}, u32[]{:S(2)}) collective-permute-start(bf16[8,5248]{1,0:T(8,128)(2,1)S(1)} %pad_maximum_fusion.1), channel_id=1, source_target_pairs={{0,4},{1,5},{2,6},{3,7},{4,0},{5,1},{6,2},{7,3},{8,12},{9,13},{10,... | collective-permute-start | bytes 251912 | tf_op jit(solution)/shard_map/ppermute | solution.py:339
  17.2 7.2 %collective-permute-start.5 = (bf16[16,5248]{1,0:T(8,128)(2,1)S(1)}, bf16[16,5248]{1,0:T(8,128)(2,1)S(1)}, u32[]{:S(2)}, u32[]{:S(2)}) collective-permute-start(bf16[16,5248]{1,0:T(8,128)(2,1)S(1)} %pad_maximum_fusion.refs_0_), channel_id=1, source_target_pairs={{0,16},{1,17},{2,18},{3,19},{4,20},{5,21},{6,22},{7,23},{8,24},{9,... | collective-permute-start | bytes 503816 | tf_op jit(solution)/shard_map/ppermute | solution.py:339
  17.8 9.5 %collective-permute-start.6 = (bf16[16,5248]{1,0:T(8,128)(2,1)S(1)}, bf16[16,5248]{1,0:T(8,128)(2,1)S(1)}, u32[]{:S(2)}, u32[]{:S(2)}) collective-permute-start(bf16[16,5248]{1,0:T(8,128)(2,1)S(1)} %pad_maximum_fusion.refs_0_), channel_id=1, source_target_pairs={{0,2},{1,3},{2,0},{3,1},{4,6},{5,7},{6,4},{7,5},{8,10},{9,11},{10,... | collective-permute-start | bytes 503816 | tf_op jit(solution)/shard_map/ppermute | solution.py:339
  18.3 9.0 %collective-permute-start.7 = (bf16[16,5248]{1,0:T(8,128)(2,1)S(1)}, bf16[16,5248]{1,0:T(8,128)(2,1)S(1)}, u32[]{:S(2)}, u32[]{:S(2)}) collective-permute-start(bf16[16,5248]{1,0:T(8,128)(2,1)S(1)} %pad_maximum_fusion.refs_0_), channel_id=1, source_target_pairs={{0,18},{1,19},{2,16},{3,17},{4,22},{5,23},{6,20},{7,21},{8,26},{9,... | collective-permute-start | bytes 503816 | tf_op jit(solution)/shard_map/ppermute | solution.py:339
  20.8 7.0 %collective-permute-start.12 = (bf16[16,2560]{1,0:T(8,128)(2,1)S(1)}, bf16[16,2560]{1,0:T(8,128)(2,1)S(1)}, u32[]{:S(2)}, u32[]{:S(2)}) collective-permute-start(bf16[16,2560]{1,0:T(8,128)(2,1)S(1)} %constant_dynamic-update-slice_fusion.first_ref), channel_id=1, source_target_pairs={{0,8},{1,9},{2,10},{3,11},{4,12},{5,13},{6,14},{7,15},{8,0},{9,1},... | collective-permute-start | bytes 245768 | tf_op jit(solution)/shard_map/ppermute | solution.py:339
  21.1 7.5 %collective-permute-start.8 = (bf16[16,5248]{1,0:T(8,128)(2,1)S(1)}, bf16[16,5248]{1,0:T(8,128)(2,1)S(1)}, u32[]{:S(2)}, u32[]{:S(2)}) collective-permute-start(bf16[16,5248]{1,0:T(8,128)(2,1)S(1)} %pad_maximum_fusion.refs_0_), channel_id=1, source_target_pairs={{0,1},{1,0},{2,3},{3,2},{4,5},{5,4},{6,7},{7,6},{8,9},{9,8},{10,11... | collective-permute-start | bytes 503816 | tf_op jit(solution)/shard_map/ppermute | solution.py:339
  24.4 4.1 %collective-permute-start.9 = (bf16[16,5248]{1,0:T(8,128)(2,1)S(1)}, bf16[16,5248]{1,0:T(8,128)(2,1)S(1)}, u32[]{:S(2)}, u32[]{:S(2)}) collective-permute-start(bf16[16,5248]{1,0:T(8,128)(2,1)S(1)} %collective-permute-done.5.refs_1_), channel_id=1, source_target_pairs={{0,1},{1,0},{2,3},{3,2},{4,5},{5,4},{6,7},{7,6},{8,9},{9,8},{10,11... | collective-permute-start | bytes 503816 | tf_op jit(solution)/shard_map/ppermute | solution.py:339
  27.3 1.4 %collective-permute-start.10 = (bf16[16,5248]{1,0:T(8,128)(2,1)S(1)}, bf16[16,5248]{1,0:T(8,128)(2,1)S(1)}, u32[]{:S(2)}, u32[]{:S(2)}) collective-permute-start(bf16[16,5248]{1,0:T(8,128)(2,1)S(1)} %collective-permute-done.6.refs_2_), channel_id=1, source_target_pairs={{0,1},{1,0},{2,3},{3,2},{4,5},{5,4},{6,7},{7,6},{8,9},{9,8},{10,11... | collective-permute-start | bytes 503816 | tf_op jit(solution)/shard_map/ppermute | solution.py:339
  27.3 1.6 %collective-permute-start.11 = (bf16[16,5248]{1,0:T(8,128)(2,1)S(1)}, bf16[16,5248]{1,0:T(8,128)(2,1)S(1)}, u32[]{:S(2)}, u32[]{:S(2)}) collective-permute-start(bf16[16,5248]{1,0:T(8,128)(2,1)S(1)} %collective-permute-done.7.refs_3_), channel_id=1, source_target_pairs={{0,1},{1,0},{2,3},{3,2},{4,5},{5,4},{6,7},{7,6},{8,9},{9,8},{10,11... | collective-permute-start | bytes 503816 | tf_op jit(solution)/shard_map/ppermute | solution.py:339
  27.8 6.2 %collective-permute-start.13 = (bf16[32,2560]{1,0:T(8,128)(2,1)S(1)}, bf16[32,2560]{1,0:T(8,128)(2,1)S(1)}, u32[]{:S(2)}, u32[]{:S(2)}) collective-permute-start(bf16[32,2560]{1,0:T(8,128)(2,1)S(1)} %join.1), channel_id=1, source_target_pairs={{0,4},{1,5},{2,6},{3,7},{4,0},{5,1},{6,2},{7,3},{8,12},{9,13},{10,... | collective-permute-start | bytes 491528 | tf_op jit(solution)/shard_map/ppermute | solution.py:339
  34.0 12.3 %collective-permute-start.15 = (bf16[64,2560]{1,0:T(8,128)(2,1)S(1)}, bf16[64,2560]{1,0:T(8,128)(2,1)S(1)}, u32[]{:S(2)}, u32[]{:S(2)}) collective-permute-start(bf16[64,2560]{1,0:T(8,128)(2,1)S(1)} %constant_dynamic-update-slice_fusion.2.up_near), channel_id=1, source_target_pairs={{0,1},{1,0},{2,3},{3,2},{4,5},{5,4},{6,7},{7,6},{8,9},{9,8},{10,11... | collective-permute-start | bytes 983048 | tf_op jit(solution)/shard_map/ppermute | solution.py:339
  45.0 1.3 %collective-permute-start.14 = (bf16[16,16,128]{2,1,0:T(8,128)(2,1)S(1)}, bf16[16,16,128]{2,1,0:T(8,128)(2,1)S(1)}, u32[]{:S(2)}, u32[]{:S(2)}) collective-permute-start(bf16[16,16,128]{2,1,0:T(8,128)(2,1)S(1)} %all_to_all.5.near_ref), channel_id=1, source_target_pairs={{0,1},{1,0},{2,3},{3,2},{4,5},{5,4},{6,7},{7,6},{8,9},{9,8},{10,11... | collective-permute-start | bytes 196616 | tf_op jit(solution)/shard_map/ppermute | solution.py:339

commit v3 on v2

--- a/solution.py
+++ b/solution.py
@@ -210,15 +210,14 @@
 
 
 def hidden_kernel(step, pieces, *refs):
-    x_refs = refs[:pieces]
-    early_w, early_v, late_w, late_v, own_up, other_up = refs[pieces : pieces + 6]
-    hid_ref, low_ref, cross_ref, gate_ref, x_all = refs[pieces + 6 :]
+    x_refs = refs[:pieces][::-1]
+    early_w, early_v, late_w, late_v = refs[pieces : pieces + 4]
+    hid_ref, low_ref, gate_ref, x_all = refs[pieces + 4 :]
     at = 0
     for ref in x_refs:
         x_all[pl.ds(at, ref.shape[0]), :] = ref[...]
         at += ref.shape[0]
     width = early_w.shape[2]
-    half = width // 2
     x = x_all[:, pl.ds(0, width)]
     low = jnp.zeros(low_ref.shape, f32)
     base = 0
@@ -231,10 +230,6 @@
             low = low + dot(v_ref[:, pl.ds(at, step)], hidden, 1, 0)
         base += w_ref.shape[1]
 
-    dp = lax.axis_index("dp")
-    here = pl.ds(pl.multiple_of(dp * half, 128), half)
-    there = pl.ds(pl.multiple_of((1 - dp) * half, 128), half)
-    cross_ref[...] = dot(own_up[...], x_all[:, here], 1, 1) + dot(other_up[...], x_all[:, there], 1, 1)
     lane = lax.broadcasted_iota(jnp.int32, (16, 128), 1)
     row = lax.broadcasted_iota(jnp.int32, (16, 128), 0)
     mine = ((lane & 15) == (own_number() & 15)) & (lane < 48)
@@ -253,6 +248,20 @@
     block = jnp.concatenate([ordered, products], axis=0).astype(bf16)
     for i in range(send_ref.shape[0]):
         send_ref[i] = block
+
+
+def table_kernel(x_all, own_up, other_up, gate_ref, cross_ref, factors_ref, order_ref):
+    tokens = x_all.shape[0]
+    half = own_up.shape[1]
+    dp = lax.axis_index("dp")
+    here = pl.ds(pl.multiple_of(dp * half, 128), half)
+    there = pl.ds(pl.multiple_of((1 - dp) * half, 128), half)
+    cross_ref[...] = dot(own_up[...], x_all[:, here], 1, 1) + dot(other_up[...], x_all[:, there], 1, 1)
+    lane = lax.broadcasted_iota(jnp.int32, (tokens, tokens), 1)
+    row = lax.broadcasted_iota(jnp.int32, (tokens, tokens), 0)
+    mate = (lane & ~3) | gate_ref[8:9].astype(jnp.int32)
+    factors_ref[...] = control * ((row == mate).astype(f32) - (row == lane).astype(f32)).astype(bf16)
+    order_ref[...] = order_table(tokens)
 
 
 def gradient_kernel(
@@ -266,6 +275,8 @@
     gram_ref,
     cross_ref,
     gate_ref,
+    apart_ref,
+    order_ref,
     down_out,
     up_out,
     blocks_buf,
@@ -280,7 +291,7 @@
         away = ((b & 1) << 0) | (((b >> 1) & 1) << 2) | (((b >> 2) & 1) << 1)
         source = far_ref if (b >> 3) & 1 else near_ref
         blocks_buf[b] = source[(dp ^ (b >> 4)) * chips + (chip ^ away)]
-    local = dot(blocks_buf[...].reshape(blocks * 16, tokens), order_table(tokens), 1, 0)
+    local = dot(blocks_buf[...].reshape(blocks * 16, tokens), order_ref[...], 1, 0)
     local = local.reshape(2, 16, 16, tokens)[:, :, 0:8]
     lows = (local[0] + local[1]).reshape(tokens, tokens)
     own_low = low_ref[...] + local[1, 0]
@@ -290,31 +301,33 @@
         [gram_ref[...] + ends[0][:, :near_rows], ends[1][:, near_rows:] + ends[2][:, near_rows:]], axis=1
     )
 
-    gates = gate_ref[...]
-    lane = lax.broadcasted_iota(jnp.int32, (tokens, tokens), 1)
-    row = lax.broadcasted_iota(jnp.int32, (tokens, tokens), 0)
-    mate = (lane & ~3) | gates[8:9].astype(jnp.int32)
-    apart = (row == lane).astype(f32) - (row == mate).astype(f32)
-    factors = jnp.concatenate([adapter_scale * lows, -control * apart], axis=0)
-    scale = 2.0 / math.sqrt(tokens)
-
-    mixed = dot(own_low, factors, 1, 1, highest_precision)
-    high, low = split_two((adapter_scale * scale) * mixed)
-    both = jnp.concatenate([high, low], axis=0)
+    scale = 2.0 * adapter_scale / math.sqrt(tokens)
+    lows_high, lows_low = split_two(adapter_scale * lows)
+    apart = apart_ref[...]
+
+    def three(left, high, low, dim):
+        left_high, left_low = split_two(left)
+        both = dot(jnp.concatenate([left_high, left_low], axis=0), high, 1, dim)
+        return both[0:8] + both[8:16] + dot(left_high, low, 1, dim)
+
+    def two(left, right, dim):
+        both = dot(jnp.concatenate(split_two(left), axis=0), right, 1, dim)
+        return both[0:8] + both[8:16]
+
+    mixed = scale * three(own_low, lows_high, lows_low, 1)
+    mixed_x = scale * two(own_low, apart, 1)
     here = pl.ds(pl.multiple_of(dp * half, 128), half)
+    mixed = jnp.concatenate(split_two(mixed), axis=0)
+    mixed_x = jnp.concatenate(split_two(mixed_x), axis=0)
     up = (
-        dot(both[:, :near_rows], up_near[...], 1, 0)
-        + dot(both[:, near_rows:tokens], up_far[...], 1, 0)
-        + dot(both[:, tokens:], x_all[:, here], 1, 0)
+        dot(mixed[:, :near_rows], up_near[...], 1, 0)
+        + dot(mixed[:, near_rows:], up_far[...], 1, 0)
+        + dot(mixed_x, x_all[:, here], 1, 0)
     )
     up_out[...] = up[0:8] + up[8:16]
 
-    products = jnp.concatenate([gram, cross_ref[...]], axis=1)
-    cot_low = dot(products, factors, 1, 0, highest_precision) * gates[0:8]
-    high, low = split_two((adapter_scale * scale) * cot_low)
-    both = jnp.concatenate([high, low], axis=0)
-    down = dot(both, hid_ref[...], 1, 1)
-    down_out[...] = down[0:8] + down[8:16]
+    cot_low = three(gram, lows_high, lows_low, 0) + two(cross_ref[...], apart, 0)
+    down_out[...] = two(scale * gate_ref[0:8] * cot_low, hid_ref[...], 1)
 
 
 def dense_body(
@@ -347,9 +360,6 @@
     def after(values, other):
         return lax.optimization_barrier((values, other))[0]
 
-    def after(value, other):
-        return lax.optimization_barrier((value, other))[0]
-
     column, own_up = pl.pallas_call(
         start_kernel,
         out_shape=(
@@ -381,13 +391,12 @@
             name=name,
         )(stay(w), stay(v))
 
-    weights = fetch(0, "fetch_early", column)
     first = grow(column, 8)
     other_up, sibling, ups = swap(own_up, 16), swap(own_up, 1), swap(own_up, 2)
-    first, weights, other_up, sibling, ups = lax.optimization_barrier((first, weights, other_up, sibling, ups))
-    late_weights = fetch(units // 2, "fetch_late", first)
+    weights = fetch(0, "fetch_early", first)
     column = grow(first, 4)
-    column, late_weights = lax.optimization_barrier((column, late_weights))
+    column, weights, other_up, sibling, ups = lax.optimization_barrier((column, weights, other_up, sibling, ups))
+    late_weights = fetch(units // 2, "fetch_late", column)
     ups = jnp.concatenate([own_up, ups], axis=0)
     third = swap(ups, 8)
     near = [swap(column, 16), swap(column, 2), swap(column, 18)]
@@ -401,25 +410,26 @@
         name="join",
     )(*after((ups, third), column))
     fourth = swap(ups, 4)
+    near, late_weights = lax.optimization_barrier((near[::-1], late_weights))
+    near = near[::-1]
     near = [column] + near
     pieces = near + [swap(piece, 1) for piece in near]
 
     count = len(pieces)
-    hidden, low, cross, gates, everything = pl.pallas_call(
+    hidden, low, gates, everything = pl.pallas_call(
         functools.partial(hidden_kernel, units // 4, count),
         out_shape=(
             pltpu.VMEM((units, total), bf16),
             pltpu.VMEM((rank, total), f32),
-            pltpu.VMEM((rank, total), f32),
             pltpu.VMEM((16, total), f32),
             pltpu.VMEM((total, width + 128), bf16),
         ),
-        in_specs=[vmem] * (count + 6),
-        out_specs=(vmem,) * 5,
+        in_specs=[vmem] * (count + 4),
+        out_specs=(vmem,) * 4,
         compiler_params=pltpu.CompilerParams(vmem_limit_bytes=8 * mib),
         cost_estimate=pl.CostEstimate(flops=0, bytes_accessed=16 * mib, transcendentals=0),
         name="hidden",
-    )(*pieces, *weights, *late_weights, own_up, other_up)
+    )(*pieces[::-1], *weights, *late_weights)
 
     up_near = jnp.concatenate(after((ups, fourth), low), axis=0)
     up_far = swap(up_near, 1)
@@ -438,19 +448,33 @@
     from_near = lax.all_to_all(send, ("dp", "chip"), split_axis=0, concat_axis=0, tiled=True)
     from_far = swap(from_near, 1)
 
+    cross, apart, order = pl.pallas_call(
+        table_kernel,
+        out_shape=(
+            pltpu.VMEM((rank, total), f32),
+            pltpu.VMEM((total, total), bf16),
+            pltpu.VMEM((total, total), bf16),
+        ),
+        in_specs=[vmem] * 4,
+        out_specs=(vmem,) * 3,
+        compiler_params=pltpu.CompilerParams(vmem_limit_bytes=4 * mib),
+        cost_estimate=pl.CostEstimate(flops=0, bytes_accessed=4 * mib, transcendentals=0),
+        name="table",
+    )(everything, own_up, other_up, after(gates, from_near))
+
     down, up = pl.pallas_call(
         gradient_kernel,
         out_shape=(
             jax.ShapeDtypeStruct((rank, units), f32),
             jax.ShapeDtypeStruct((rank, half), f32),
         ),
-        in_specs=[vmem] * 10,
+        in_specs=[vmem] * 12,
         out_specs=(vmem, vmem),
         scratch_shapes=[pltpu.VMEM((devices, 16, total), bf16)],
         compiler_params=pltpu.CompilerParams(vmem_limit_bytes=16 * mib),
         name="gradient",
     )(
-        from_near, from_far, up_near, up_far, everything, hidden, low, gram, cross, gates
+        from_near, from_far, up_near, up_far, everything, hidden, low, gram, cross, gates, apart, order
     )
     return (down[None], up[None])
 

time: 48.2 us -> 45.9 us (0.952)
  waiting for transfers between devices: 7.93 us -> 2.7 us
  starting transfers between devices: 14.2 us -> 16 us
  blocking collectives: 10.4 us -> 11.3 us
    ppermute x16, waiting for transfers between devices: 7.93 us -> 2.7 us  [swap(): return lax.ppermute(value, every, [(i, i ^ mask) for i in range(devices)])]
    ppermute x16, starting transfers between devices: 14.2 us -> 16 us  [swap(): return lax.ppermute(value, every, [(i, i ^ mask) for i in range(devices)])]
    all_to_all x1, blocking collectives: 10.4 us -> 11.3 us  [dense_body(): lax.all_to_all(send, ('dp', 'chip'), split_axis=0, concat_axis=0, tiled=T...]
  transfers between devices with their start and end apart: 16 -> 16, of which waited for: 6 -> 5; matrix products, arithmetic and copies ran while one was open for 0% -> 0% of each run, Pallas kernels for 24% -> 26%
where the time goes in v3:
time: 45.9 us; the launch traced here: 45.6 us
  starting transfers between devices  16 us (35%)
  Pallas kernels  14.7 us (32%)
  blocking collectives  11.3 us (25%)
  waiting for transfers between devices  2.7 us (6%)
  between operations  0.74 us (2%)
    ppermute x16, starting transfers between devices, swap(): return lax.ppermute(value, every, [(i, i ^ mask) for i in range(devices)])  16 us
    all_to_all x1, blocking collectives, dense_body(): lax.all_to_all(send, ('dp', 'chip'), split_axis=0, concat_axis=0, tiled=T...  11.3 us
    pallas_call x2, Pallas kernels, fetch(): pl.pallas_call(functools.partial(fetch_kernel, first), out_shape=(pltpu.V...  6.72 us
    pallas_call x1, Pallas kernels, dense_body(): pl.pallas_call(functools.partial(hidden_kernel, units // 4, count), out_s...  4.72 us
    ppermute x16, waiting for transfers between devices, swap(): return lax.ppermute(value, every, [(i, i ^ mask) for i in range(devices)])  2.7 us
    pallas_call x1, Pallas kernels, dense_body(): pl.pallas_call(gradient_kernel, out_shape=(jax.ShapeDtypeStruct((rank, un...  1.49 us
    pallas_call x1, Pallas kernels, dense_body(): pl.pallas_call(start_kernel, out_shape=(pltpu.VMEM((tok_count, width + 12...  0.94 us
  transfers between devices with their start and end apart: 16, of which 5 were waited for; matrix products, arithmetic and copies ran while one was open for 0% of the time, Pallas kernels for 26%

profile of v3, /device:TPU:0, one launch (start us, length us, event | category | flops | bytes accessed | tf_op | source)
XLA Modules:
  0.0 45.6 jit_solution(11479236430357209995)
XLA Ops:
  0.6 0.9 %start.1 = (bf16[4,5248]{1,0:T(4,128)(2,1)S(1)}, bf16[8,2560]{1,0:T(8,128)(2,1)S(1)}) custom-call(bf16[4,5120]{1,0:T(4,128)(2,1)} %x_ref.1, bf16[8,2560]{1,0:T(8,128)(2,1)} %bitcast.9, s32[4,6]{1,0:T(4,128)} %index_ref.1, f32[4,6]{1,0:T(4,128)} %gate_ref.1, s32[4]{0:T(128)} %partner_ref.1), custom_call_target="tpu_custom_call" | custom-call | tf_op jit(solution)/shard_map/start/pallas_call | solution.py:363
  1.6 4.1 %collective-permute-start = (bf16[4,5248]{1,0:T(4,128)(2,1)S(1)}, bf16[4,5248]{1,0:T(4,128)(2,1)S(1)}, u32[]{:S(2)}, u32[]{:S(2)}) collective-permute-start(bf16[4,5248]{1,0:T(4,128)(2,1)S(1)} %get-tuple-element.39), channel_id=1, source_target_pairs={{0,8},{1,9},{2,10},{3,11},{4,12},{5,13},{6,14},{7,15},{8,0},{9,1},... | collective-permute-start | bytes 125960 | tf_op jit(solution)/shard_map/ppermute | solution.py:352
  5.7 1.5 %collective-permute-start.2 = (bf16[8,2560]{1,0:T(8,128)(2,1)S(1)}, bf16[8,2560]{1,0:T(8,128)(2,1)S(1)}, u32[]{:S(2)}, u32[]{:S(2)}) collective-permute-start(bf16[8,2560]{1,0:T(8,128)(2,1)S(1)} %get-tuple-element.44.own_up), channel_id=1, source_target_pairs={{0,16},{1,17},{2,18},{3,19},{4,20},{5,21},{6,22},{7,23},{8,24},{9,... | collective-permute-start | bytes 122888 | tf_op jit(solution)/shard_map/ppermute | solution.py:352
  7.2 0.0 collective-permute-start.3
  7.2 1.5 %collective-permute-start.4 = (bf16[8,2560]{1,0:T(8,128)(2,1)S(1)}, bf16[8,2560]{1,0:T(8,128)(2,1)S(1)}, u32[]{:S(2)}, u32[]{:S(2)}) collective-permute-start(bf16[8,2560]{1,0:T(8,128)(2,1)S(1)} %get-tuple-element.44.own_up), channel_id=1, source_target_pairs={{0,2},{1,3},{2,0},{3,1},{4,6},{5,7},{6,4},{7,5},{8,10},{9,11},{10,... | collective-permute-start | bytes 122888 | tf_op jit(solution)/shard_map/ppermute | solution.py:352
  8.7 0.0 collective-permute-done
  8.7 1.6 %collective-permute-start.1 = (bf16[8,5248]{1,0:T(8,128)(2,1)S(1)}, bf16[8,5248]{1,0:T(8,128)(2,1)S(1)}, u32[]{:S(2)}, u32[]{:S(2)}) collective-permute-start(bf16[8,5248]{1,0:T(8,128)(2,1)S(1)} %pad_maximum_fusion.1), channel_id=1, source_target_pairs={{0,4},{1,5},{2,6},{3,7},{4,0},{5,1},{6,2},{7,3},{8,12},{9,13},{10,... | collective-permute-start | bytes 251912 | tf_op jit(solution)/shard_map/ppermute | solution.py:352
  10.4 3.4 %fetch_early.1 = (bf16[2,384,5120]{2,1,0:T(8,128)(2,1)S(1)}, bf16[8,384]{1,0:T(8,128)(2,1)S(1)}) custom-call(bf16[2,768,5120]{2,1,0:T(8,128)(2,1)} %bitcast.5, bf16[8,768]{1,0:T(8,128)(2,1)} %bitcast.7), custom_call_target="tpu_custom_call" | custom-call | bytes 8388608 | tf_op jit(solution)/shard_map/fetch_early/pallas_call | solution.py:383
  13.8 0.0 collective-permute-done.1
  13.8 0.1 pad_maximum_fusion.refs_7_
  13.9 0.0 collective-permute-done.2.other_up
  13.9 0.0 collective-permute-done.4
  13.9 1.8 %collective-permute-start.5 = (bf16[16,5248]{1,0:T(8,128)(2,1)S(1)}, bf16[16,5248]{1,0:T(8,128)(2,1)S(1)}, u32[]{:S(2)}, u32[]{:S(2)}) collective-permute-start(bf16[16,5248]{1,0:T(8,128)(2,1)S(1)} %pad_maximum_fusion.refs_7_), channel_id=1, source_target_pairs={{0,18},{1,19},{2,16},{3,17},{4,22},{5,23},{6,20},{7,21},{8,26},{9,... | collective-permute-start | bytes 503816 | tf_op jit(solution)/shard_map/ppermute | solution.py:352
  15.7 0.5 %collective-permute-start.6 = (bf16[16,5248]{1,0:T(8,128)(2,1)S(1)}, bf16[16,5248]{1,0:T(8,128)(2,1)S(1)}, u32[]{:S(2)}, u32[]{:S(2)}) collective-permute-start(bf16[16,5248]{1,0:T(8,128)(2,1)S(1)} %pad_maximum_fusion.refs_7_), channel_id=1, source_target_pairs={{0,2},{1,3},{2,0},{3,1},{4,6},{5,7},{6,4},{7,5},{8,10},{9,11},{10,... | collective-permute-start | bytes 503816 | tf_op jit(solution)/shard_map/ppermute | solution.py:352
  16.2 1.2 %collective-permute-start.7 = (bf16[16,5248]{1,0:T(8,128)(2,1)S(1)}, bf16[16,5248]{1,0:T(8,128)(2,1)S(1)}, u32[]{:S(2)}, u32[]{:S(2)}) collective-permute-start(bf16[16,5248]{1,0:T(8,128)(2,1)S(1)} %pad_maximum_fusion.refs_7_), channel_id=1, source_target_pairs={{0,16},{1,17},{2,18},{3,19},{4,20},{5,21},{6,22},{7,23},{8,24},{9,... | collective-permute-start | bytes 503816 | tf_op jit(solution)/shard_map/ppermute | solution.py:352
  17.4 2.2 %collective-permute-start.12 = (bf16[16,2560]{1,0:T(8,128)(2,1)S(1)}, bf16[16,2560]{1,0:T(8,128)(2,1)S(1)}, u32[]{:S(2)}, u32[]{:S(2)}) collective-permute-start(bf16[16,2560]{1,0:T(8,128)(2,1)S(1)} %constant_dynamic-update-slice_fusion.first_ref), channel_id=1, source_target_pairs={{0,8},{1,9},{2,10},{3,11},{4,12},{5,13},{6,14},{7,15},{8,0},{9,1},... | collective-permute-start | bytes 245768 | tf_op jit(solution)/shard_map/ppermute | solution.py:352
  19.7 0.0 collective-permute-start.11
  19.7 3.4 %fetch_late.1 = (bf16[2,384,5120]{2,1,0:T(8,128)(2,1)S(1)}, bf16[8,384]{1,0:T(8,128)(2,1)S(1)}) custom-call(bf16[2,768,5120]{2,1,0:T(8,128)(2,1)} %bitcast.6, bf16[8,768]{1,0:T(8,128)(2,1)} %bitcast.8), custom_call_target="tpu_custom_call" | custom-call | bytes 8388608 | tf_op jit(solution)/shard_map/fetch_late/pallas_call | solution.py:383
  23.1 0.8 %collective-permute-done.6.refs_5_ = bf16[16,5248]{1,0:T(8,128)(2,1)S(1)} collective-permute-done((bf16[16,5248]{1,0:T(8,128)(2,1)S(1)}, bf16[16,5248]{1,0:T(8,128)(2,1)S(1)}, u32[]{:S(2)}, u32[]{:S(2)}) %collective-permute-start.6) | collective-permute-done | bytes 167968 | tf_op jit(solution)/shard_map/ppermute | solution.py:352
  23.9 0.5 %collective-permute-start.9 = (bf16[16,5248]{1,0:T(8,128)(2,1)S(1)}, bf16[16,5248]{1,0:T(8,128)(2,1)S(1)}, u32[]{:S(2)}, u32[]{:S(2)}) collective-permute-start(bf16[16,5248]{1,0:T(8,128)(2,1)S(1)} %collective-permute-done.6.refs_5_), channel_id=1, source_target_pairs={{0,1},{1,0},{2,3},{3,2},{4,5},{5,4},{6,7},{7,6},{8,9},{9,8},{10,11... | collective-permute-start | bytes 503816 | tf_op jit(solution)/shard_map/ppermute | solution.py:352
  24.4 0.0 collective-permute-start.10
  24.4 0.9 %collective-permute-start.13 = (bf16[32,2560]{1,0:T(8,128)(2,1)S(1)}, bf16[32,2560]{1,0:T(8,128)(2,1)S(1)}, u32[]{:S(2)}, u32[]{:S(2)}) collective-permute-start(bf16[32,2560]{1,0:T(8,128)(2,1)S(1)} %join.1), channel_id=1, source_target_pairs={{0,4},{1,5},{2,6},{3,7},{4,0},{5,1},{6,2},{7,3},{8,12},{9,13},{10,... | collective-permute-start | bytes 491528 | tf_op jit(solution)/shard_map/ppermute | solution.py:352
  25.3 0.2 collective-permute-done.9.refs_1_
  25.5 0.3 collective-permute-done.10.refs_2_
  25.8 4.7 %hidden.1 = (bf16[768,128]{1,0:T(8,128)(2,1)S(1)}, f32[8,128]{1,0:T(8,128)S(1)}, f32[16,128]{1,0:T(8,128)S(1)}, bf16[128,5248]{1,0:T(8,128)(2,1)S(1)}) custom-call(bf16[16,5248]{1,0:T(8,128)(2,1)S(1)} %collective-permute-done.8.refs_0_, bf16[16,5248]{1,0:T(8,128)(2,1)S(1)} %collective-permute-done.9.refs_1_, ...), custom_call_target="tpu_custom_call" | custom-call | bytes 16777216 | tf_op jit(solution)/shard_map/hidden/pallas_call | solution.py:419
  30.5 0.6 %collective-permute-done.13 = bf16[32,2560]{1,0:T(8,128)(2,1)S(1)} collective-permute-done((bf16[32,2560]{1,0:T(8,128)(2,1)S(1)}, bf16[32,2560]{1,0:T(8,128)(2,1)S(1)}, u32[]{:S(2)}, u32[]{:S(2)}) %collective-permute-start.13) | collective-permute-done | bytes 163872 | tf_op jit(solution)/shard_map/ppermute | solution.py:352
  31.1 0.1 collective-permute-start.15
  31.2 0.4 send.1
  31.6 11.3 %all_to_all.5.near_ref = bf16[16,16,128]{2,1,0:T(8,128)(2,1)S(1)} all-to-all(bf16[16,16,128]{2,1,0:T(8,128)(2,1)S(1)} %get-tuple-element.64), channel_id=1, replica_groups=mesh['dp'=2,'chip'=8,'core'=2] {'dp','chip'}, dimensions={0} | all-to-all | bytes 131072 | tf_op jit(solution)/shard_map/all_to_all | solution.py:448
  42.9 0.5 %table.1 = (f32[8,128]{1,0:T(8,128)S(1)}, bf16[128,128]{1,0:T(8,128)(2,1)S(1)}, bf16[128,128]{1,0:T(8,128)(2,1)S(1)}) custom-call(bf16[128,5248]{1,0:T(8,128)(2,1)S(1)} %get-tuple-element.65.x_all, bf16[8,2560]{1,0:T(8,128)(2,1)S(1)} %get-tuple-element.44.own_up, bf16[8,2560]{1,0:T(8,128)(2,1)S(1)} %collective-permute-done.2.other_up, ...), custom_call_target="tpu_custom_call" | custom-call | bytes 4194304 | tf_op jit(solution)/shard_map/table/pallas_call | solution.py:451
  43.4 0.8 %collective-permute-done.14.far_ref = bf16[16,16,128]{2,1,0:T(8,128)(2,1)S(1)} collective-permute-done((bf16[16,16,128]{2,1,0:T(8,128)(2,1)S(1)}, bf16[16,16,128]{2,1,0:T(8,128)(2,1)S(1)}, u32[]{:S(2)}, u32[]{:S(2)}) %collective-permute-start.14) | collective-permute-done | bytes 65568 | tf_op jit(solution)/shard_map/ppermute | solution.py:352
  44.1 1.5 %gradient.1 = (f32[8,768]{1,0:T(8,128)}, f32[8,2560]{1,0:T(8,128)}) custom-call(bf16[16,16,128]{2,1,0:T(8,128)(2,1)S(1)} %all_to_all.5.near_ref, bf16[16,16,128]{2,1,0:T(8,128)(2,1)S(1)} %collective-permute-done.14.far_ref, bf16[64,2560]{1,0:T(8,128)(2,1)S(1)} %constant_dynamic-update-slice_fusion.2.up_near, ...), custom_call_target="tpu_custom_call" | custom-call | tf_op jit(solution)/shard_map/gradient/pallas_call | solution.py:465
  (15 shorter events, 0.1 us)
Async XLA Ops:
  1.6 7.1 %collective-permute-start = (bf16[4,5248]{1,0:T(4,128)(2,1)S(1)}, bf16[4,5248]{1,0:T(4,128)(2,1)S(1)}, u32[]{:S(2)}, u32[]{:S(2)}) collective-permute-start(bf16[4,5248]{1,0:T(4,128)(2,1)S(1)} %get-tuple-element.39), channel_id=1, source_target_pairs={{0,8},{1,9},{2,10},{3,11},{4,12},{5,13},{6,14},{7,15},{8,0},{9,1},... | collective-permute-start | bytes 125960 | tf_op jit(solution)/shard_map/ppermute | solution.py:352
  5.7 8.2 %collective-permute-start.2 = (bf16[8,2560]{1,0:T(8,128)(2,1)S(1)}, bf16[8,2560]{1,0:T(8,128)(2,1)S(1)}, u32[]{:S(2)}, u32[]{:S(2)}) collective-permute-start(bf16[8,2560]{1,0:T(8,128)(2,1)S(1)} %get-tuple-element.44.own_up), channel_id=1, source_target_pairs={{0,16},{1,17},{2,18},{3,19},{4,20},{5,21},{6,22},{7,23},{8,24},{9,... | collective-permute-start | bytes 122888 | tf_op jit(solution)/shard_map/ppermute | solution.py:352
  7.2 6.7 %collective-permute-start.3 = (bf16[8,2560]{1,0:T(8,128)(2,1)S(1)}, bf16[8,2560]{1,0:T(8,128)(2,1)S(1)}, u32[]{:S(2)}, u32[]{:S(2)}) collective-permute-start(bf16[8,2560]{1,0:T(8,128)(2,1)S(1)} %get-tuple-element.44.own_up), channel_id=1, source_target_pairs={{0,1},{1,0},{2,3},{3,2},{4,5},{5,4},{6,7},{7,6},{8,9},{9,8},{10,11... | collective-permute-start | bytes 122888 | tf_op jit(solution)/shard_map/ppermute | solution.py:352
  7.2 6.7 %collective-permute-start.4 = (bf16[8,2560]{1,0:T(8,128)(2,1)S(1)}, bf16[8,2560]{1,0:T(8,128)(2,1)S(1)}, u32[]{:S(2)}, u32[]{:S(2)}) collective-permute-start(bf16[8,2560]{1,0:T(8,128)(2,1)S(1)} %get-tuple-element.44.own_up), channel_id=1, source_target_pairs={{0,2},{1,3},{2,0},{3,1},{4,6},{5,7},{6,4},{7,5},{8,10},{9,11},{10,... | collective-permute-start | bytes 122888 | tf_op jit(solution)/shard_map/ppermute | solution.py:352
  8.7 5.0 %collective-permute-start.1 = (bf16[8,5248]{1,0:T(8,128)(2,1)S(1)}, bf16[8,5248]{1,0:T(8,128)(2,1)S(1)}, u32[]{:S(2)}, u32[]{:S(2)}) collective-permute-start(bf16[8,5248]{1,0:T(8,128)(2,1)S(1)} %pad_maximum_fusion.1), channel_id=1, source_target_pairs={{0,4},{1,5},{2,6},{3,7},{4,0},{5,1},{6,2},{7,3},{8,12},{9,13},{10,... | collective-permute-start | bytes 251912 | tf_op jit(solution)/shard_map/ppermute | solution.py:352
  13.9 9.2 %collective-permute-start.5 = (bf16[16,5248]{1,0:T(8,128)(2,1)S(1)}, bf16[16,5248]{1,0:T(8,128)(2,1)S(1)}, u32[]{:S(2)}, u32[]{:S(2)}) collective-permute-start(bf16[16,5248]{1,0:T(8,128)(2,1)S(1)} %pad_maximum_fusion.refs_7_), channel_id=1, source_target_pairs={{0,18},{1,19},{2,16},{3,17},{4,22},{5,23},{6,20},{7,21},{8,26},{9,... | collective-permute-start | bytes 503816 | tf_op jit(solution)/shard_map/ppermute | solution.py:352
  15.7 8.2 %collective-permute-start.6 = (bf16[16,5248]{1,0:T(8,128)(2,1)S(1)}, bf16[16,5248]{1,0:T(8,128)(2,1)S(1)}, u32[]{:S(2)}, u32[]{:S(2)}) collective-permute-start(bf16[16,5248]{1,0:T(8,128)(2,1)S(1)} %pad_maximum_fusion.refs_7_), channel_id=1, source_target_pairs={{0,2},{1,3},{2,0},{3,1},{4,6},{5,7},{6,4},{7,5},{8,10},{9,11},{10,... | collective-permute-start | bytes 503816 | tf_op jit(solution)/shard_map/ppermute | solution.py:352
  16.2 7.7 %collective-permute-start.7 = (bf16[16,5248]{1,0:T(8,128)(2,1)S(1)}, bf16[16,5248]{1,0:T(8,128)(2,1)S(1)}, u32[]{:S(2)}, u32[]{:S(2)}) collective-permute-start(bf16[16,5248]{1,0:T(8,128)(2,1)S(1)} %pad_maximum_fusion.refs_7_), channel_id=1, source_target_pairs={{0,16},{1,17},{2,18},{3,19},{4,20},{5,21},{6,22},{7,23},{8,24},{9,... | collective-permute-start | bytes 503816 | tf_op jit(solution)/shard_map/ppermute | solution.py:352
  17.4 7.0 %collective-permute-start.12 = (bf16[16,2560]{1,0:T(8,128)(2,1)S(1)}, bf16[16,2560]{1,0:T(8,128)(2,1)S(1)}, u32[]{:S(2)}, u32[]{:S(2)}) collective-permute-start(bf16[16,2560]{1,0:T(8,128)(2,1)S(1)} %constant_dynamic-update-slice_fusion.first_ref), channel_id=1, source_target_pairs={{0,8},{1,9},{2,10},{3,11},{4,12},{5,13},{6,14},{7,15},{8,0},{9,1},... | collective-permute-start | bytes 245768 | tf_op jit(solution)/shard_map/ppermute | solution.py:352
  19.7 5.7 %collective-permute-start.11 = (bf16[16,5248]{1,0:T(8,128)(2,1)S(1)}, bf16[16,5248]{1,0:T(8,128)(2,1)S(1)}, u32[]{:S(2)}, u32[]{:S(2)}) collective-permute-start(bf16[16,5248]{1,0:T(8,128)(2,1)S(1)} %pad_maximum_fusion.refs_7_), channel_id=1, source_target_pairs={{0,1},{1,0},{2,3},{3,2},{4,5},{5,4},{6,7},{7,6},{8,9},{9,8},{10,11... | collective-permute-start | bytes 503816 | tf_op jit(solution)/shard_map/ppermute | solution.py:352
  23.9 1.4 %collective-permute-start.8 = (bf16[16,5248]{1,0:T(8,128)(2,1)S(1)}, bf16[16,5248]{1,0:T(8,128)(2,1)S(1)}, u32[]{:S(2)}, u32[]{:S(2)}) collective-permute-start(bf16[16,5248]{1,0:T(8,128)(2,1)S(1)} %collective-permute-done.5.refs_4_), channel_id=1, source_target_pairs={{0,1},{1,0},{2,3},{3,2},{4,5},{5,4},{6,7},{7,6},{8,9},{9,8},{10,11... | collective-permute-start | bytes 503816 | tf_op jit(solution)/shard_map/ppermute | solution.py:352
  23.9 1.6 %collective-permute-start.9 = (bf16[16,5248]{1,0:T(8,128)(2,1)S(1)}, bf16[16,5248]{1,0:T(8,128)(2,1)S(1)}, u32[]{:S(2)}, u32[]{:S(2)}) collective-permute-start(bf16[16,5248]{1,0:T(8,128)(2,1)S(1)} %collective-permute-done.6.refs_5_), channel_id=1, source_target_pairs={{0,1},{1,0},{2,3},{3,2},{4,5},{5,4},{6,7},{7,6},{8,9},{9,8},{10,11... | collective-permute-start | bytes 503816 | tf_op jit(solution)/shard_map/ppermute | solution.py:352
  24.4 1.4 %collective-permute-start.10 = (bf16[16,5248]{1,0:T(8,128)(2,1)S(1)}, bf16[16,5248]{1,0:T(8,128)(2,1)S(1)}, u32[]{:S(2)}, u32[]{:S(2)}) collective-permute-start(bf16[16,5248]{1,0:T(8,128)(2,1)S(1)} %collective-permute-done.7.refs_6_), channel_id=1, source_target_pairs={{0,1},{1,0},{2,3},{3,2},{4,5},{5,4},{6,7},{7,6},{8,9},{9,8},{10,11... | collective-permute-start | bytes 503816 | tf_op jit(solution)/shard_map/ppermute | solution.py:352
  24.4 6.7 %collective-permute-start.13 = (bf16[32,2560]{1,0:T(8,128)(2,1)S(1)}, bf16[32,2560]{1,0:T(8,128)(2,1)S(1)}, u32[]{:S(2)}, u32[]{:S(2)}) collective-permute-start(bf16[32,2560]{1,0:T(8,128)(2,1)S(1)} %join.1), channel_id=1, source_target_pairs={{0,4},{1,5},{2,6},{3,7},{4,0},{5,1},{6,2},{7,3},{8,12},{9,13},{10,... | collective-permute-start | bytes 491528 | tf_op jit(solution)/shard_map/ppermute | solution.py:352
  31.1 13.0 %collective-permute-start.15 = (bf16[64,2560]{1,0:T(8,128)(2,1)S(1)}, bf16[64,2560]{1,0:T(8,128)(2,1)S(1)}, u32[]{:S(2)}, u32[]{:S(2)}) collective-permute-start(bf16[64,2560]{1,0:T(8,128)(2,1)S(1)} %constant_dynamic-update-slice_fusion.2.up_near), channel_id=1, source_target_pairs={{0,1},{1,0},{2,3},{3,2},{4,5},{5,4},{6,7},{7,6},{8,9},{9,8},{10,11... | collective-permute-start | bytes 983048 | tf_op jit(solution)/shard_map/ppermute | solution.py:352
  42.9 1.3 %collective-permute-start.14 = (bf16[16,16,128]{2,1,0:T(8,128)(2,1)S(1)}, bf16[16,16,128]{2,1,0:T(8,128)(2,1)S(1)}, u32[]{:S(2)}, u32[]{:S(2)}) collective-permute-start(bf16[16,16,128]{2,1,0:T(8,128)(2,1)S(1)} %all_to_all.5.near_ref), channel_id=1, source_target_pairs={{0,1},{1,0},{2,3},{3,2},{4,5},{5,4},{6,7},{7,6},{8,9},{9,8},{10,11... | collective-permute-start | bytes 196616 | tf_op jit(solution)/shard_map/ppermute | solution.py:352

commit v4 on v3

--- a/solution.py
+++ b/solution.py
@@ -223,8 +223,8 @@
     base = 0
     for w_ref, v_ref in ((early_w, early_v), (late_w, late_v)):
         for at in range(0, w_ref.shape[1], step):
-            gate = dot(w_ref[0, pl.ds(at, step), :], x, 1, 1)
-            up = dot(w_ref[1, pl.ds(at, step), :], x, 1, 1)
+            both = dot(w_ref[:, pl.ds(at, step), :].reshape(2 * step, width), x, 1, 1)
+            gate, up = both[:step], both[step:]
             hidden = (gate / (1.0 + jnp.exp(-gate)) * up).astype(bf16)
             hid_ref[pl.ds(base + at, step), :] = hidden
             low = low + dot(v_ref[:, pl.ds(at, step)], hidden, 1, 0)
@@ -417,7 +417,7 @@
 
     count = len(pieces)
     hidden, low, gates, everything = pl.pallas_call(
-        functools.partial(hidden_kernel, units // 4, count),
+        functools.partial(hidden_kernel, units // 2, count),
         out_shape=(
             pltpu.VMEM((units, total), bf16),
             pltpu.VMEM((rank, total), f32),

time: 45.9 us -> 45.9 us (level)
  transfers between devices with their start and end apart: 16 -> 16, of which waited for: 5 -> 5; matrix products, arithmetic and copies ran while one was open for 0% -> 0% of each run, Pallas kernels for 26% -> 25%
where the time goes in v4:
time: 45.9 us; the launch traced here: 45.6 us
  starting transfers between devices  16 us (35%)
  Pallas kernels  14.3 us (31%)
  blocking collectives  11.3 us (25%)
  waiting for transfers between devices  3.09 us (7%)
  between operations  0.74 us (2%)
    ppermute x16, starting transfers between devices, swap(): return lax.ppermute(value, every, [(i, i ^ mask) for i in range(devices)])  16 us
    all_to_all x1, blocking collectives, dense_body(): lax.all_to_all(send, ('dp', 'chip'), split_axis=0, concat_axis=0, tiled=T...  11.3 us
    pallas_call x2, Pallas kernels, fetch(): pl.pallas_call(functools.partial(fetch_kernel, first), out_shape=(pltpu.V...  6.72 us
    pallas_call x1, Pallas kernels, dense_body(): pl.pallas_call(functools.partial(hidden_kernel, units // 2, count), out_s...  4.33 us
    ppermute x16, waiting for transfers between devices, swap(): return lax.ppermute(value, every, [(i, i ^ mask) for i in range(devices)])  3.09 us
    pallas_call x1, Pallas kernels, dense_body(): pl.pallas_call(gradient_kernel, out_shape=(jax.ShapeDtypeStruct((rank, un...  1.49 us
    pallas_call x1, Pallas kernels, dense_body(): pl.pallas_call(start_kernel, out_shape=(pltpu.VMEM((tok_count, width + 12...  0.94 us
  transfers between devices with their start and end apart: 16, of which 5 were waited for; matrix products, arithmetic and copies ran while one was open for 0% of the time, Pallas kernels for 25%

profile of v4, /device:TPU:0, one launch (start us, length us, event | category | flops | bytes accessed | tf_op | source)
XLA Modules:
  0.0 45.6 jit_solution(6094654606140167901)
XLA Ops:
  0.6 0.9 %start.1 = (bf16[4,5248]{1,0:T(4,128)(2,1)S(1)}, bf16[8,2560]{1,0:T(8,128)(2,1)S(1)}) custom-call(bf16[4,5120]{1,0:T(4,128)(2,1)} %x_ref.1, bf16[8,2560]{1,0:T(8,128)(2,1)} %bitcast.9, s32[4,6]{1,0:T(4,128)} %index_ref.1, f32[4,6]{1,0:T(4,128)} %gate_ref.1, s32[4]{0:T(128)} %partner_ref.1), custom_call_target="tpu_custom_call" | custom-call | tf_op jit(solution)/shard_map/start/pallas_call | solution.py:363
  1.6 4.1 %collective-permute-start = (bf16[4,5248]{1,0:T(4,128)(2,1)S(1)}, bf16[4,5248]{1,0:T(4,128)(2,1)S(1)}, u32[]{:S(2)}, u32[]{:S(2)}) collective-permute-start(bf16[4,5248]{1,0:T(4,128)(2,1)S(1)} %get-tuple-element.39), channel_id=1, source_target_pairs={{0,8},{1,9},{2,10},{3,11},{4,12},{5,13},{6,14},{7,15},{8,0},{9,1},... | collective-permute-start | bytes 125960 | tf_op jit(solution)/shard_map/ppermute | solution.py:352
  5.7 1.5 %collective-permute-start.2 = (bf16[8,2560]{1,0:T(8,128)(2,1)S(1)}, bf16[8,2560]{1,0:T(8,128)(2,1)S(1)}, u32[]{:S(2)}, u32[]{:S(2)}) collective-permute-start(bf16[8,2560]{1,0:T(8,128)(2,1)S(1)} %get-tuple-element.44.own_up), channel_id=1, source_target_pairs={{0,16},{1,17},{2,18},{3,19},{4,20},{5,21},{6,22},{7,23},{8,24},{9,... | collective-permute-start | bytes 122888 | tf_op jit(solution)/shard_map/ppermute | solution.py:352
  7.2 0.0 collective-permute-start.3
  7.2 1.5 %collective-permute-start.4 = (bf16[8,2560]{1,0:T(8,128)(2,1)S(1)}, bf16[8,2560]{1,0:T(8,128)(2,1)S(1)}, u32[]{:S(2)}, u32[]{:S(2)}) collective-permute-start(bf16[8,2560]{1,0:T(8,128)(2,1)S(1)} %get-tuple-element.44.own_up), channel_id=1, source_target_pairs={{0,2},{1,3},{2,0},{3,1},{4,6},{5,7},{6,4},{7,5},{8,10},{9,11},{10,... | collective-permute-start | bytes 122888 | tf_op jit(solution)/shard_map/ppermute | solution.py:352
  8.7 0.0 collective-permute-done
  8.7 1.6 %collective-permute-start.1 = (bf16[8,5248]{1,0:T(8,128)(2,1)S(1)}, bf16[8,5248]{1,0:T(8,128)(2,1)S(1)}, u32[]{:S(2)}, u32[]{:S(2)}) collective-permute-start(bf16[8,5248]{1,0:T(8,128)(2,1)S(1)} %pad_maximum_fusion.1), channel_id=1, source_target_pairs={{0,4},{1,5},{2,6},{3,7},{4,0},{5,1},{6,2},{7,3},{8,12},{9,13},{10,... | collective-permute-start | bytes 251912 | tf_op jit(solution)/shard_map/ppermute | solution.py:352
  10.4 3.4 %fetch_early.1 = (bf16[2,384,5120]{2,1,0:T(8,128)(2,1)S(1)}, bf16[8,384]{1,0:T(8,128)(2,1)S(1)}) custom-call(bf16[2,768,5120]{2,1,0:T(8,128)(2,1)} %bitcast.5, bf16[8,768]{1,0:T(8,128)(2,1)} %bitcast.7), custom_call_target="tpu_custom_call" | custom-call | bytes 8388608 | tf_op jit(solution)/shard_map/fetch_early/pallas_call | solution.py:383
  13.8 0.0 collective-permute-done.1
  13.8 0.1 pad_maximum_fusion.refs_7_
  13.9 0.0 collective-permute-done.2.other_up
  13.9 0.0 collective-permute-done.4
  13.9 1.8 %collective-permute-start.5 = (bf16[16,5248]{1,0:T(8,128)(2,1)S(1)}, bf16[16,5248]{1,0:T(8,128)(2,1)S(1)}, u32[]{:S(2)}, u32[]{:S(2)}) collective-permute-start(bf16[16,5248]{1,0:T(8,128)(2,1)S(1)} %pad_maximum_fusion.refs_7_), channel_id=1, source_target_pairs={{0,18},{1,19},{2,16},{3,17},{4,22},{5,23},{6,20},{7,21},{8,26},{9,... | collective-permute-start | bytes 503816 | tf_op jit(solution)/shard_map/ppermute | solution.py:352
  15.7 0.5 %collective-permute-start.6 = (bf16[16,5248]{1,0:T(8,128)(2,1)S(1)}, bf16[16,5248]{1,0:T(8,128)(2,1)S(1)}, u32[]{:S(2)}, u32[]{:S(2)}) collective-permute-start(bf16[16,5248]{1,0:T(8,128)(2,1)S(1)} %pad_maximum_fusion.refs_7_), channel_id=1, source_target_pairs={{0,2},{1,3},{2,0},{3,1},{4,6},{5,7},{6,4},{7,5},{8,10},{9,11},{10,... | collective-permute-start | bytes 503816 | tf_op jit(solution)/shard_map/ppermute | solution.py:352
  16.2 1.2 %collective-permute-start.7 = (bf16[16,5248]{1,0:T(8,128)(2,1)S(1)}, bf16[16,5248]{1,0:T(8,128)(2,1)S(1)}, u32[]{:S(2)}, u32[]{:S(2)}) collective-permute-start(bf16[16,5248]{1,0:T(8,128)(2,1)S(1)} %pad_maximum_fusion.refs_7_), channel_id=1, source_target_pairs={{0,16},{1,17},{2,18},{3,19},{4,20},{5,21},{6,22},{7,23},{8,24},{9,... | collective-permute-start | bytes 503816 | tf_op jit(solution)/shard_map/ppermute | solution.py:352
  17.4 2.2 %collective-permute-start.12 = (bf16[16,2560]{1,0:T(8,128)(2,1)S(1)}, bf16[16,2560]{1,0:T(8,128)(2,1)S(1)}, u32[]{:S(2)}, u32[]{:S(2)}) collective-permute-start(bf16[16,2560]{1,0:T(8,128)(2,1)S(1)} %constant_dynamic-update-slice_fusion.first_ref), channel_id=1, source_target_pairs={{0,8},{1,9},{2,10},{3,11},{4,12},{5,13},{6,14},{7,15},{8,0},{9,1},... | collective-permute-start | bytes 245768 | tf_op jit(solution)/shard_map/ppermute | solution.py:352
  19.7 0.0 collective-permute-start.11
  19.7 3.4 %fetch_late.1 = (bf16[2,384,5120]{2,1,0:T(8,128)(2,1)S(1)}, bf16[8,384]{1,0:T(8,128)(2,1)S(1)}) custom-call(bf16[2,768,5120]{2,1,0:T(8,128)(2,1)} %bitcast.6, bf16[8,768]{1,0:T(8,128)(2,1)} %bitcast.8), custom_call_target="tpu_custom_call" | custom-call | bytes 8388608 | tf_op jit(solution)/shard_map/fetch_late/pallas_call | solution.py:383
  23.1 0.8 %collective-permute-done.6.refs_5_ = bf16[16,5248]{1,0:T(8,128)(2,1)S(1)} collective-permute-done((bf16[16,5248]{1,0:T(8,128)(2,1)S(1)}, bf16[16,5248]{1,0:T(8,128)(2,1)S(1)}, u32[]{:S(2)}, u32[]{:S(2)}) %collective-permute-start.6) | collective-permute-done | bytes 167968 | tf_op jit(solution)/shard_map/ppermute | solution.py:352
  23.9 0.5 %collective-permute-start.9 = (bf16[16,5248]{1,0:T(8,128)(2,1)S(1)}, bf16[16,5248]{1,0:T(8,128)(2,1)S(1)}, u32[]{:S(2)}, u32[]{:S(2)}) collective-permute-start(bf16[16,5248]{1,0:T(8,128)(2,1)S(1)} %collective-permute-done.6.refs_5_), channel_id=1, source_target_pairs={{0,1},{1,0},{2,3},{3,2},{4,5},{5,4},{6,7},{7,6},{8,9},{9,8},{10,11... | collective-permute-start | bytes 503816 | tf_op jit(solution)/shard_map/ppermute | solution.py:352
  24.4 0.0 collective-permute-start.10
  24.4 0.9 %collective-permute-start.13 = (bf16[32,2560]{1,0:T(8,128)(2,1)S(1)}, bf16[32,2560]{1,0:T(8,128)(2,1)S(1)}, u32[]{:S(2)}, u32[]{:S(2)}) collective-permute-start(bf16[32,2560]{1,0:T(8,128)(2,1)S(1)} %join.1), channel_id=1, source_target_pairs={{0,4},{1,5},{2,6},{3,7},{4,0},{5,1},{6,2},{7,3},{8,12},{9,13},{10,... | collective-permute-start | bytes 491528 | tf_op jit(solution)/shard_map/ppermute | solution.py:352
  25.3 0.2 collective-permute-done.9.refs_1_
  25.5 0.3 collective-permute-done.10.refs_2_
  25.8 4.3 %hidden.1 = (bf16[768,128]{1,0:T(8,128)(2,1)S(1)}, f32[8,128]{1,0:T(8,128)S(1)}, f32[16,128]{1,0:T(8,128)S(1)}, bf16[128,5248]{1,0:T(8,128)(2,1)S(1)}) custom-call(bf16[16,5248]{1,0:T(8,128)(2,1)S(1)} %collective-permute-done.8.refs_0_, bf16[16,5248]{1,0:T(8,128)(2,1)S(1)} %collective-permute-done.9.refs_1_, ...), custom_call_target="tpu_custom_call" | custom-call | bytes 16777216 | tf_op jit(solution)/shard_map/hidden/pallas_call | solution.py:419
  30.1 1.0 %collective-permute-done.13 = bf16[32,2560]{1,0:T(8,128)(2,1)S(1)} collective-permute-done((bf16[32,2560]{1,0:T(8,128)(2,1)S(1)}, bf16[32,2560]{1,0:T(8,128)(2,1)S(1)}, u32[]{:S(2)}, u32[]{:S(2)}) %collective-permute-start.13) | collective-permute-done | bytes 163872 | tf_op jit(solution)/shard_map/ppermute | solution.py:352
  31.1 0.1 collective-permute-start.15
  31.2 0.4 send.1
  31.6 11.3 %all_to_all.5.near_ref = bf16[16,16,128]{2,1,0:T(8,128)(2,1)S(1)} all-to-all(bf16[16,16,128]{2,1,0:T(8,128)(2,1)S(1)} %get-tuple-element.64), channel_id=1, replica_groups=mesh['dp'=2,'chip'=8,'core'=2] {'dp','chip'}, dimensions={0} | all-to-all | bytes 131072 | tf_op jit(solution)/shard_map/all_to_all | solution.py:448
  42.9 0.5 %table.1 = (f32[8,128]{1,0:T(8,128)S(1)}, bf16[128,128]{1,0:T(8,128)(2,1)S(1)}, bf16[128,128]{1,0:T(8,128)(2,1)S(1)}) custom-call(bf16[128,5248]{1,0:T(8,128)(2,1)S(1)} %get-tuple-element.65.x_all, bf16[8,2560]{1,0:T(8,128)(2,1)S(1)} %get-tuple-element.44.own_up, bf16[8,2560]{1,0:T(8,128)(2,1)S(1)} %collective-permute-done.2.other_up, ...), custom_call_target="tpu_custom_call" | custom-call | bytes 4194304 | tf_op jit(solution)/shard_map/table/pallas_call | solution.py:451
  43.3 0.8 %collective-permute-done.14.far_ref = bf16[16,16,128]{2,1,0:T(8,128)(2,1)S(1)} collective-permute-done((bf16[16,16,128]{2,1,0:T(8,128)(2,1)S(1)}, bf16[16,16,128]{2,1,0:T(8,128)(2,1)S(1)}, u32[]{:S(2)}, u32[]{:S(2)}) %collective-permute-start.14) | collective-permute-done | bytes 65568 | tf_op jit(solution)/shard_map/ppermute | solution.py:352
  44.1 1.5 %gradient.1 = (f32[8,768]{1,0:T(8,128)}, f32[8,2560]{1,0:T(8,128)}) custom-call(bf16[16,16,128]{2,1,0:T(8,128)(2,1)S(1)} %all_to_all.5.near_ref, bf16[16,16,128]{2,1,0:T(8,128)(2,1)S(1)} %collective-permute-done.14.far_ref, bf16[64,2560]{1,0:T(8,128)(2,1)S(1)} %constant_dynamic-update-slice_fusion.2.up_near, ...), custom_call_target="tpu_custom_call" | custom-call | tf_op jit(solution)/shard_map/gradient/pallas_call | solution.py:465
  (15 shorter events, 0.1 us)
Async XLA Ops:
  1.6 7.1 %collective-permute-start = (bf16[4,5248]{1,0:T(4,128)(2,1)S(1)}, bf16[4,5248]{1,0:T(4,128)(2,1)S(1)}, u32[]{:S(2)}, u32[]{:S(2)}) collective-permute-start(bf16[4,5248]{1,0:T(4,128)(2,1)S(1)} %get-tuple-element.39), channel_id=1, source_target_pairs={{0,8},{1,9},{2,10},{3,11},{4,12},{5,13},{6,14},{7,15},{8,0},{9,1},... | collective-permute-start | bytes 125960 | tf_op jit(solution)/shard_map/ppermute | solution.py:352
  5.7 8.2 %collective-permute-start.2 = (bf16[8,2560]{1,0:T(8,128)(2,1)S(1)}, bf16[8,2560]{1,0:T(8,128)(2,1)S(1)}, u32[]{:S(2)}, u32[]{:S(2)}) collective-permute-start(bf16[8,2560]{1,0:T(8,128)(2,1)S(1)} %get-tuple-element.44.own_up), channel_id=1, source_target_pairs={{0,16},{1,17},{2,18},{3,19},{4,20},{5,21},{6,22},{7,23},{8,24},{9,... | collective-permute-start | bytes 122888 | tf_op jit(solution)/shard_map/ppermute | solution.py:352
  7.2 6.7 %collective-permute-start.3 = (bf16[8,2560]{1,0:T(8,128)(2,1)S(1)}, bf16[8,2560]{1,0:T(8,128)(2,1)S(1)}, u32[]{:S(2)}, u32[]{:S(2)}) collective-permute-start(bf16[8,2560]{1,0:T(8,128)(2,1)S(1)} %get-tuple-element.44.own_up), channel_id=1, source_target_pairs={{0,1},{1,0},{2,3},{3,2},{4,5},{5,4},{6,7},{7,6},{8,9},{9,8},{10,11... | collective-permute-start | bytes 122888 | tf_op jit(solution)/shard_map/ppermute | solution.py:352
  7.2 6.7 %collective-permute-start.4 = (bf16[8,2560]{1,0:T(8,128)(2,1)S(1)}, bf16[8,2560]{1,0:T(8,128)(2,1)S(1)}, u32[]{:S(2)}, u32[]{:S(2)}) collective-permute-start(bf16[8,2560]{1,0:T(8,128)(2,1)S(1)} %get-tuple-element.44.own_up), channel_id=1, source_target_pairs={{0,2},{1,3},{2,0},{3,1},{4,6},{5,7},{6,4},{7,5},{8,10},{9,11},{10,... | collective-permute-start | bytes 122888 | tf_op jit(solution)/shard_map/ppermute | solution.py:352
  8.7 5.0 %collective-permute-start.1 = (bf16[8,5248]{1,0:T(8,128)(2,1)S(1)}, bf16[8,5248]{1,0:T(8,128)(2,1)S(1)}, u32[]{:S(2)}, u32[]{:S(2)}) collective-permute-start(bf16[8,5248]{1,0:T(8,128)(2,1)S(1)} %pad_maximum_fusion.1), channel_id=1, source_target_pairs={{0,4},{1,5},{2,6},{3,7},{4,0},{5,1},{6,2},{7,3},{8,12},{9,13},{10,... | collective-permute-start | bytes 251912 | tf_op jit(solution)/shard_map/ppermute | solution.py:352
  13.9 9.2 %collective-permute-start.5 = (bf16[16,5248]{1,0:T(8,128)(2,1)S(1)}, bf16[16,5248]{1,0:T(8,128)(2,1)S(1)}, u32[]{:S(2)}, u32[]{:S(2)}) collective-permute-start(bf16[16,5248]{1,0:T(8,128)(2,1)S(1)} %pad_maximum_fusion.refs_7_), channel_id=1, source_target_pairs={{0,18},{1,19},{2,16},{3,17},{4,22},{5,23},{6,20},{7,21},{8,26},{9,... | collective-permute-start | bytes 503816 | tf_op jit(solution)/shard_map/ppermute | solution.py:352
  15.7 8.2 %collective-permute-start.6 = (bf16[16,5248]{1,0:T(8,128)(2,1)S(1)}, bf16[16,5248]{1,0:T(8,128)(2,1)S(1)}, u32[]{:S(2)}, u32[]{:S(2)}) collective-permute-start(bf16[16,5248]{1,0:T(8,128)(2,1)S(1)} %pad_maximum_fusion.refs_7_), channel_id=1, source_target_pairs={{0,2},{1,3},{2,0},{3,1},{4,6},{5,7},{6,4},{7,5},{8,10},{9,11},{10,... | collective-permute-start | bytes 503816 | tf_op jit(solution)/shard_map/ppermute | solution.py:352
  16.2 7.7 %collective-permute-start.7 = (bf16[16,5248]{1,0:T(8,128)(2,1)S(1)}, bf16[16,5248]{1,0:T(8,128)(2,1)S(1)}, u32[]{:S(2)}, u32[]{:S(2)}) collective-permute-start(bf16[16,5248]{1,0:T(8,128)(2,1)S(1)} %pad_maximum_fusion.refs_7_), channel_id=1, source_target_pairs={{0,16},{1,17},{2,18},{3,19},{4,20},{5,21},{6,22},{7,23},{8,24},{9,... | collective-permute-start | bytes 503816 | tf_op jit(solution)/shard_map/ppermute | solution.py:352
  17.4 7.0 %collective-permute-start.12 = (bf16[16,2560]{1,0:T(8,128)(2,1)S(1)}, bf16[16,2560]{1,0:T(8,128)(2,1)S(1)}, u32[]{:S(2)}, u32[]{:S(2)}) collective-permute-start(bf16[16,2560]{1,0:T(8,128)(2,1)S(1)} %constant_dynamic-update-slice_fusion.first_ref), channel_id=1, source_target_pairs={{0,8},{1,9},{2,10},{3,11},{4,12},{5,13},{6,14},{7,15},{8,0},{9,1},... | collective-permute-start | bytes 245768 | tf_op jit(solution)/shard_map/ppermute | solution.py:352
  19.7 5.7 %collective-permute-start.11 = (bf16[16,5248]{1,0:T(8,128)(2,1)S(1)}, bf16[16,5248]{1,0:T(8,128)(2,1)S(1)}, u32[]{:S(2)}, u32[]{:S(2)}) collective-permute-start(bf16[16,5248]{1,0:T(8,128)(2,1)S(1)} %pad_maximum_fusion.refs_7_), channel_id=1, source_target_pairs={{0,1},{1,0},{2,3},{3,2},{4,5},{5,4},{6,7},{7,6},{8,9},{9,8},{10,11... | collective-permute-start | bytes 503816 | tf_op jit(solution)/shard_map/ppermute | solution.py:352
  23.9 1.4 %collective-permute-start.8 = (bf16[16,5248]{1,0:T(8,128)(2,1)S(1)}, bf16[16,5248]{1,0:T(8,128)(2,1)S(1)}, u32[]{:S(2)}, u32[]{:S(2)}) collective-permute-start(bf16[16,5248]{1,0:T(8,128)(2,1)S(1)} %collective-permute-done.5.refs_4_), channel_id=1, source_target_pairs={{0,1},{1,0},{2,3},{3,2},{4,5},{5,4},{6,7},{7,6},{8,9},{9,8},{10,11... | collective-permute-start | bytes 503816 | tf_op jit(solution)/shard_map/ppermute | solution.py:352
  23.9 1.6 %collective-permute-start.9 = (bf16[16,5248]{1,0:T(8,128)(2,1)S(1)}, bf16[16,5248]{1,0:T(8,128)(2,1)S(1)}, u32[]{:S(2)}, u32[]{:S(2)}) collective-permute-start(bf16[16,5248]{1,0:T(8,128)(2,1)S(1)} %collective-permute-done.6.refs_5_), channel_id=1, source_target_pairs={{0,1},{1,0},{2,3},{3,2},{4,5},{5,4},{6,7},{7,6},{8,9},{9,8},{10,11... | collective-permute-start | bytes 503816 | tf_op jit(solution)/shard_map/ppermute | solution.py:352
  24.4 1.4 %collective-permute-start.10 = (bf16[16,5248]{1,0:T(8,128)(2,1)S(1)}, bf16[16,5248]{1,0:T(8,128)(2,1)S(1)}, u32[]{:S(2)}, u32[]{:S(2)}) collective-permute-start(bf16[16,5248]{1,0:T(8,128)(2,1)S(1)} %collective-permute-done.7.refs_6_), channel_id=1, source_target_pairs={{0,1},{1,0},{2,3},{3,2},{4,5},{5,4},{6,7},{7,6},{8,9},{9,8},{10,11... | collective-permute-start | bytes 503816 | tf_op jit(solution)/shard_map/ppermute | solution.py:352
  24.4 6.7 %collective-permute-start.13 = (bf16[32,2560]{1,0:T(8,128)(2,1)S(1)}, bf16[32,2560]{1,0:T(8,128)(2,1)S(1)}, u32[]{:S(2)}, u32[]{:S(2)}) collective-permute-start(bf16[32,2560]{1,0:T(8,128)(2,1)S(1)} %join.1), channel_id=1, source_target_pairs={{0,4},{1,5},{2,6},{3,7},{4,0},{5,1},{6,2},{7,3},{8,12},{9,13},{10,... | collective-permute-start | bytes 491528 | tf_op jit(solution)/shard_map/ppermute | solution.py:352
  31.1 13.0 %collective-permute-start.15 = (bf16[64,2560]{1,0:T(8,128)(2,1)S(1)}, bf16[64,2560]{1,0:T(8,128)(2,1)S(1)}, u32[]{:S(2)}, u32[]{:S(2)}) collective-permute-start(bf16[64,2560]{1,0:T(8,128)(2,1)S(1)} %constant_dynamic-update-slice_fusion.2.up_near), channel_id=1, source_target_pairs={{0,1},{1,0},{2,3},{3,2},{4,5},{5,4},{6,7},{7,6},{8,9},{9,8},{10,11... | collective-permute-start | bytes 983048 | tf_op jit(solution)/shard_map/ppermute | solution.py:352
  42.9 1.3 %collective-permute-start.14 = (bf16[16,16,128]{2,1,0:T(8,128)(2,1)S(1)}, bf16[16,16,128]{2,1,0:T(8,128)(2,1)S(1)}, u32[]{:S(2)}, u32[]{:S(2)}) collective-permute-start(bf16[16,16,128]{2,1,0:T(8,128)(2,1)S(1)} %all_to_all.5.near_ref), channel_id=1, source_target_pairs={{0,1},{1,0},{2,3},{3,2},{4,5},{5,4},{6,7},{7,6},{8,9},{9,8},{10,11... | collective-permute-start | bytes 196616 | tf_op jit(solution)/shard_map/ppermute | solution.py:352

commit v5 on v4

--- a/solution.py
+++ b/solution.py
@@ -212,7 +212,7 @@
 def hidden_kernel(step, pieces, *refs):
     x_refs = refs[:pieces][::-1]
     early_w, early_v, late_w, late_v = refs[pieces : pieces + 4]
-    hid_ref, low_ref, gate_ref, x_all = refs[pieces + 4 :]
+    hid_ref, low_ref, ordered_ref, gate_ref, x_all = refs[pieces + 4 :]
     at = 0
     for ref in x_refs:
         x_all[pl.ds(at, ref.shape[0]), :] = ref[...]
@@ -236,16 +236,16 @@
     pick = jnp.where(row < 8, mine.astype(f32), (lane == 48).astype(f32)).astype(bf16)
     gates = dot(pick, x_all[:, pl.ds(width, 128)], 1, 1)
     gate_ref[...] = gates
-    low_ref[...] = low * gates[0:8]
-
-
-def send_kernel(low_ref, up_near, sibling_ref, gram_ref, send_ref):
-    count = low_ref.shape[1]
+    low = low * gates[0:8]
+    low_ref[...] = low
+    ordered_ref[...] = dot(low.astype(bf16), order_table(x.shape[0]), 1, 1)
+
+
+def send_kernel(ordered_ref, up_near, sibling_ref, gram_ref, send_ref):
     gram_ref[...] = dot(up_near[0:8, :], up_near[...], 1, 1)
     other = dot(sibling_ref[...], up_near[...], 1, 1)
-    ordered = dot(low_ref[...].astype(bf16), order_table(count), 1, 1)
     products = jnp.concatenate([gram_ref[...], other], axis=1)
-    block = jnp.concatenate([ordered, products], axis=0).astype(bf16)
+    block = jnp.concatenate([ordered_ref[...], products], axis=0).astype(bf16)
     for i in range(send_ref.shape[0]):
         send_ref[i] = block
 
@@ -416,16 +416,17 @@
     pieces = near + [swap(piece, 1) for piece in near]
 
     count = len(pieces)
-    hidden, low, gates, everything = pl.pallas_call(
+    hidden, low, ordered, gates, everything = pl.pallas_call(
         functools.partial(hidden_kernel, units // 2, count),
         out_shape=(
             pltpu.VMEM((units, total), bf16),
+            pltpu.VMEM((rank, total), f32),
             pltpu.VMEM((rank, total), f32),
             pltpu.VMEM((16, total), f32),
             pltpu.VMEM((total, width + 128), bf16),
         ),
         in_specs=[vmem] * (count + 4),
-        out_specs=(vmem,) * 4,
+        out_specs=(vmem,) * 5,
         compiler_params=pltpu.CompilerParams(vmem_limit_bytes=8 * mib),
         cost_estimate=pl.CostEstimate(flops=0, bytes_accessed=16 * mib, transcendentals=0),
         name="hidden",
@@ -443,7 +444,7 @@
         out_specs=(vmem,) * 2,
         compiler_params=pltpu.CompilerParams(vmem_limit_bytes=4 * mib),
         name="send",
-    )(low, up_near, sibling)
+    )(ordered, up_near, sibling)
 
     from_near = lax.all_to_all(send, ("dp", "chip"), split_axis=0, concat_axis=0, tiled=True)
     from_far = swap(from_near, 1)

time: 45.9 us -> 45.9 us (level)
  no operation moved by 1% of the time
where the time goes in v5:
time: 45.9 us; the launch traced here: 45.6 us
  starting transfers between devices  16 us (35%)
  Pallas kernels  14.4 us (31%)
  blocking collectives  11.3 us (25%)
  waiting for transfers between devices  2.99 us (7%)
  between operations  0.74 us (2%)
    ppermute x16, starting transfers between devices, swap(): return lax.ppermute(value, every, [(i, i ^ mask) for i in range(devices)])  16 us
    all_to_all x1, blocking collectives, dense_body(): lax.all_to_all(send, ('dp', 'chip'), split_axis=0, concat_axis=0, tiled=T...  11.3 us
    pallas_call x2, Pallas kernels, fetch(): pl.pallas_call(functools.partial(fetch_kernel, first), out_shape=(pltpu.V...  6.72 us
    pallas_call x1, Pallas kernels, dense_body(): pl.pallas_call(functools.partial(hidden_kernel, units // 2, count), out_s...  4.43 us
    ppermute x16, waiting for transfers between devices, swap(): return lax.ppermute(value, every, [(i, i ^ mask) for i in range(devices)])  2.99 us
    pallas_call x1, Pallas kernels, dense_body(): pl.pallas_call(gradient_kernel, out_shape=(jax.ShapeDtypeStruct((rank, un...  1.49 us
    pallas_call x1, Pallas kernels, dense_body(): pl.pallas_call(start_kernel, out_shape=(pltpu.VMEM((tok_count, width + 12...  0.94 us
  transfers between devices with their start and end apart: 16, of which 5 were waited for; matrix products, arithmetic and copies ran while one was open for 0% of the time, Pallas kernels for 25%

profile of v5, /device:TPU:0, one launch (start us, length us, event | category | flops | bytes accessed | tf_op | source)
XLA Modules:
  0.0 45.6 jit_solution(12935760687496820478)
XLA Ops:
  0.6 0.9 %start.1 = (bf16[4,5248]{1,0:T(4,128)(2,1)S(1)}, bf16[8,2560]{1,0:T(8,128)(2,1)S(1)}) custom-call(bf16[4,5120]{1,0:T(4,128)(2,1)} %x_ref.1, bf16[8,2560]{1,0:T(8,128)(2,1)} %bitcast.9, s32[4,6]{1,0:T(4,128)} %index_ref.1, f32[4,6]{1,0:T(4,128)} %gate_ref.1, s32[4]{0:T(128)} %partner_ref.1), custom_call_target="tpu_custom_call" | custom-call | tf_op jit(solution)/shard_map/start/pallas_call | solution.py:363
  1.6 4.1 %collective-permute-start = (bf16[4,5248]{1,0:T(4,128)(2,1)S(1)}, bf16[4,5248]{1,0:T(4,128)(2,1)S(1)}, u32[]{:S(2)}, u32[]{:S(2)}) collective-permute-start(bf16[4,5248]{1,0:T(4,128)(2,1)S(1)} %get-tuple-element.40), channel_id=1, source_target_pairs={{0,8},{1,9},{2,10},{3,11},{4,12},{5,13},{6,14},{7,15},{8,0},{9,1},... | collective-permute-start | bytes 125960 | tf_op jit(solution)/shard_map/ppermute | solution.py:352
  5.7 1.5 %collective-permute-start.2 = (bf16[8,2560]{1,0:T(8,128)(2,1)S(1)}, bf16[8,2560]{1,0:T(8,128)(2,1)S(1)}, u32[]{:S(2)}, u32[]{:S(2)}) collective-permute-start(bf16[8,2560]{1,0:T(8,128)(2,1)S(1)} %get-tuple-element.45.own_up), channel_id=1, source_target_pairs={{0,16},{1,17},{2,18},{3,19},{4,20},{5,21},{6,22},{7,23},{8,24},{9,... | collective-permute-start | bytes 122888 | tf_op jit(solution)/shard_map/ppermute | solution.py:352
  7.2 0.0 collective-permute-start.3
  7.2 1.5 %collective-permute-start.4 = (bf16[8,2560]{1,0:T(8,128)(2,1)S(1)}, bf16[8,2560]{1,0:T(8,128)(2,1)S(1)}, u32[]{:S(2)}, u32[]{:S(2)}) collective-permute-start(bf16[8,2560]{1,0:T(8,128)(2,1)S(1)} %get-tuple-element.45.own_up), channel_id=1, source_target_pairs={{0,2},{1,3},{2,0},{3,1},{4,6},{5,7},{6,4},{7,5},{8,10},{9,11},{10,... | collective-permute-start | bytes 122888 | tf_op jit(solution)/shard_map/ppermute | solution.py:352
  8.7 0.0 collective-permute-done
  8.7 1.6 %collective-permute-start.1 = (bf16[8,5248]{1,0:T(8,128)(2,1)S(1)}, bf16[8,5248]{1,0:T(8,128)(2,1)S(1)}, u32[]{:S(2)}, u32[]{:S(2)}) collective-permute-start(bf16[8,5248]{1,0:T(8,128)(2,1)S(1)} %pad_maximum_fusion.1), channel_id=1, source_target_pairs={{0,4},{1,5},{2,6},{3,7},{4,0},{5,1},{6,2},{7,3},{8,12},{9,13},{10,... | collective-permute-start | bytes 251912 | tf_op jit(solution)/shard_map/ppermute | solution.py:352
  10.4 3.4 %fetch_early.1 = (bf16[2,384,5120]{2,1,0:T(8,128)(2,1)S(1)}, bf16[8,384]{1,0:T(8,128)(2,1)S(1)}) custom-call(bf16[2,768,5120]{2,1,0:T(8,128)(2,1)} %bitcast.5, bf16[8,768]{1,0:T(8,128)(2,1)} %bitcast.7), custom_call_target="tpu_custom_call" | custom-call | bytes 8388608 | tf_op jit(solution)/shard_map/fetch_early/pallas_call | solution.py:383
  13.8 0.0 collective-permute-done.1
  13.8 0.1 pad_maximum_fusion.refs_7_
  13.9 0.0 collective-permute-done.2.other_up
  13.9 0.0 collective-permute-done.4
  13.9 1.8 %collective-permute-start.5 = (bf16[16,5248]{1,0:T(8,128)(2,1)S(1)}, bf16[16,5248]{1,0:T(8,128)(2,1)S(1)}, u32[]{:S(2)}, u32[]{:S(2)}) collective-permute-start(bf16[16,5248]{1,0:T(8,128)(2,1)S(1)} %pad_maximum_fusion.refs_7_), channel_id=1, source_target_pairs={{0,18},{1,19},{2,16},{3,17},{4,22},{5,23},{6,20},{7,21},{8,26},{9,... | collective-permute-start | bytes 503816 | tf_op jit(solution)/shard_map/ppermute | solution.py:352
  15.7 0.5 %collective-permute-start.6 = (bf16[16,5248]{1,0:T(8,128)(2,1)S(1)}, bf16[16,5248]{1,0:T(8,128)(2,1)S(1)}, u32[]{:S(2)}, u32[]{:S(2)}) collective-permute-start(bf16[16,5248]{1,0:T(8,128)(2,1)S(1)} %pad_maximum_fusion.refs_7_), channel_id=1, source_target_pairs={{0,2},{1,3},{2,0},{3,1},{4,6},{5,7},{6,4},{7,5},{8,10},{9,11},{10,... | collective-permute-start | bytes 503816 | tf_op jit(solution)/shard_map/ppermute | solution.py:352
  16.2 1.2 %collective-permute-start.7 = (bf16[16,5248]{1,0:T(8,128)(2,1)S(1)}, bf16[16,5248]{1,0:T(8,128)(2,1)S(1)}, u32[]{:S(2)}, u32[]{:S(2)}) collective-permute-start(bf16[16,5248]{1,0:T(8,128)(2,1)S(1)} %pad_maximum_fusion.refs_7_), channel_id=1, source_target_pairs={{0,16},{1,17},{2,18},{3,19},{4,20},{5,21},{6,22},{7,23},{8,24},{9,... | collective-permute-start | bytes 503816 | tf_op jit(solution)/shard_map/ppermute | solution.py:352
  17.4 2.2 %collective-permute-start.12 = (bf16[16,2560]{1,0:T(8,128)(2,1)S(1)}, bf16[16,2560]{1,0:T(8,128)(2,1)S(1)}, u32[]{:S(2)}, u32[]{:S(2)}) collective-permute-start(bf16[16,2560]{1,0:T(8,128)(2,1)S(1)} %constant_dynamic-update-slice_fusion.first_ref), channel_id=1, source_target_pairs={{0,8},{1,9},{2,10},{3,11},{4,12},{5,13},{6,14},{7,15},{8,0},{9,1},... | collective-permute-start | bytes 245768 | tf_op jit(solution)/shard_map/ppermute | solution.py:352
  19.7 0.0 collective-permute-start.11
  19.7 3.4 %fetch_late.1 = (bf16[2,384,5120]{2,1,0:T(8,128)(2,1)S(1)}, bf16[8,384]{1,0:T(8,128)(2,1)S(1)}) custom-call(bf16[2,768,5120]{2,1,0:T(8,128)(2,1)} %bitcast.6, bf16[8,768]{1,0:T(8,128)(2,1)} %bitcast.8), custom_call_target="tpu_custom_call" | custom-call | bytes 8388608 | tf_op jit(solution)/shard_map/fetch_late/pallas_call | solution.py:383
  23.1 0.8 %collective-permute-done.6.refs_5_ = bf16[16,5248]{1,0:T(8,128)(2,1)S(1)} collective-permute-done((bf16[16,5248]{1,0:T(8,128)(2,1)S(1)}, bf16[16,5248]{1,0:T(8,128)(2,1)S(1)}, u32[]{:S(2)}, u32[]{:S(2)}) %collective-permute-start.6) | collective-permute-done | bytes 167968 | tf_op jit(solution)/shard_map/ppermute | solution.py:352
  23.9 0.5 %collective-permute-start.9 = (bf16[16,5248]{1,0:T(8,128)(2,1)S(1)}, bf16[16,5248]{1,0:T(8,128)(2,1)S(1)}, u32[]{:S(2)}, u32[]{:S(2)}) collective-permute-start(bf16[16,5248]{1,0:T(8,128)(2,1)S(1)} %collective-permute-done.6.refs_5_), channel_id=1, source_target_pairs={{0,1},{1,0},{2,3},{3,2},{4,5},{5,4},{6,7},{7,6},{8,9},{9,8},{10,11... | collective-permute-start | bytes 503816 | tf_op jit(solution)/shard_map/ppermute | solution.py:352
  24.4 0.0 collective-permute-start.10
  24.4 0.9 %collective-permute-start.13 = (bf16[32,2560]{1,0:T(8,128)(2,1)S(1)}, bf16[32,2560]{1,0:T(8,128)(2,1)S(1)}, u32[]{:S(2)}, u32[]{:S(2)}) collective-permute-start(bf16[32,2560]{1,0:T(8,128)(2,1)S(1)} %join.1), channel_id=1, source_target_pairs={{0,4},{1,5},{2,6},{3,7},{4,0},{5,1},{6,2},{7,3},{8,12},{9,13},{10,... | collective-permute-start | bytes 491528 | tf_op jit(solution)/shard_map/ppermute | solution.py:352
  25.3 0.2 collective-permute-done.9.refs_1_
  25.5 0.3 collective-permute-done.10.refs_2_
  25.8 4.4 %hidden.1 = (bf16[768,128]{1,0:T(8,128)(2,1)S(1)}, f32[8,128]{1,0:T(8,128)S(1)}, f32[8,128]{1,0:T(8,128)S(1)}, f32[16,128]{1,0:T(8,128)S(1)}, bf16[128,5248]{1,0:T(8,128)(2,1)S(1)}) custom-call(bf16[16,5248]{1,0:T(8,128)(2,1)S(1)} %collective-permute-done.8.refs_0_, bf16[16,5248]{1,0:T(8,128)(2,1)S(1)} %collective-permute-done.9.refs_1_, ...), custom_call_target="tpu_custom_call" | custom-call | bytes 16777216 | tf_op jit(solution)/shard_map/hidden/pallas_call | solution.py:419
  30.2 0.9 %collective-permute-done.13 = bf16[32,2560]{1,0:T(8,128)(2,1)S(1)} collective-permute-done((bf16[32,2560]{1,0:T(8,128)(2,1)S(1)}, bf16[32,2560]{1,0:T(8,128)(2,1)S(1)}, u32[]{:S(2)}, u32[]{:S(2)}) %collective-permute-start.13) | collective-permute-done | bytes 163872 | tf_op jit(solution)/shard_map/ppermute | solution.py:352
  31.1 0.1 collective-permute-start.15
  31.2 0.3 send.1
  31.5 11.3 %all_to_all.5.near_ref = bf16[16,16,128]{2,1,0:T(8,128)(2,1)S(1)} all-to-all(bf16[16,16,128]{2,1,0:T(8,128)(2,1)S(1)} %get-tuple-element.66), channel_id=1, replica_groups=mesh['dp'=2,'chip'=8,'core'=2] {'dp','chip'}, dimensions={0} | all-to-all | bytes 131072 | tf_op jit(solution)/shard_map/all_to_all | solution.py:449
  42.9 0.5 %table.1 = (f32[8,128]{1,0:T(8,128)S(1)}, bf16[128,128]{1,0:T(8,128)(2,1)S(1)}, bf16[128,128]{1,0:T(8,128)(2,1)S(1)}) custom-call(bf16[128,5248]{1,0:T(8,128)(2,1)S(1)} %get-tuple-element.67.x_all, bf16[8,2560]{1,0:T(8,128)(2,1)S(1)} %get-tuple-element.45.own_up, bf16[8,2560]{1,0:T(8,128)(2,1)S(1)} %collective-permute-done.2.other_up, ...), custom_call_target="tpu_custom_call" | custom-call | bytes 4194304 | tf_op jit(solution)/shard_map/table/pallas_call | solution.py:452
  43.3 0.8 %collective-permute-done.14.far_ref = bf16[16,16,128]{2,1,0:T(8,128)(2,1)S(1)} collective-permute-done((bf16[16,16,128]{2,1,0:T(8,128)(2,1)S(1)}, bf16[16,16,128]{2,1,0:T(8,128)(2,1)S(1)}, u32[]{:S(2)}, u32[]{:S(2)}) %collective-permute-start.14) | collective-permute-done | bytes 65568 | tf_op jit(solution)/shard_map/ppermute | solution.py:352
  44.1 1.5 %gradient.1 = (f32[8,768]{1,0:T(8,128)}, f32[8,2560]{1,0:T(8,128)}) custom-call(bf16[16,16,128]{2,1,0:T(8,128)(2,1)S(1)} %all_to_all.5.near_ref, bf16[16,16,128]{2,1,0:T(8,128)(2,1)S(1)} %collective-permute-done.14.far_ref, bf16[64,2560]{1,0:T(8,128)(2,1)S(1)} %constant_dynamic-update-slice_fusion.2.up_near, ...), custom_call_target="tpu_custom_call" | custom-call | tf_op jit(solution)/shard_map/gradient/pallas_call | solution.py:466
  (15 shorter events, 0.1 us)
Async XLA Ops:
  1.6 7.1 %collective-permute-start = (bf16[4,5248]{1,0:T(4,128)(2,1)S(1)}, bf16[4,5248]{1,0:T(4,128)(2,1)S(1)}, u32[]{:S(2)}, u32[]{:S(2)}) collective-permute-start(bf16[4,5248]{1,0:T(4,128)(2,1)S(1)} %get-tuple-element.40), channel_id=1, source_target_pairs={{0,8},{1,9},{2,10},{3,11},{4,12},{5,13},{6,14},{7,15},{8,0},{9,1},... | collective-permute-start | bytes 125960 | tf_op jit(solution)/shard_map/ppermute | solution.py:352
  5.7 8.2 %collective-permute-start.2 = (bf16[8,2560]{1,0:T(8,128)(2,1)S(1)}, bf16[8,2560]{1,0:T(8,128)(2,1)S(1)}, u32[]{:S(2)}, u32[]{:S(2)}) collective-permute-start(bf16[8,2560]{1,0:T(8,128)(2,1)S(1)} %get-tuple-element.45.own_up), channel_id=1, source_target_pairs={{0,16},{1,17},{2,18},{3,19},{4,20},{5,21},{6,22},{7,23},{8,24},{9,... | collective-permute-start | bytes 122888 | tf_op jit(solution)/shard_map/ppermute | solution.py:352
  7.2 6.7 %collective-permute-start.3 = (bf16[8,2560]{1,0:T(8,128)(2,1)S(1)}, bf16[8,2560]{1,0:T(8,128)(2,1)S(1)}, u32[]{:S(2)}, u32[]{:S(2)}) collective-permute-start(bf16[8,2560]{1,0:T(8,128)(2,1)S(1)} %get-tuple-element.45.own_up), channel_id=1, source_target_pairs={{0,1},{1,0},{2,3},{3,2},{4,5},{5,4},{6,7},{7,6},{8,9},{9,8},{10,11... | collective-permute-start | bytes 122888 | tf_op jit(solution)/shard_map/ppermute | solution.py:352
  7.2 6.7 %collective-permute-start.4 = (bf16[8,2560]{1,0:T(8,128)(2,1)S(1)}, bf16[8,2560]{1,0:T(8,128)(2,1)S(1)}, u32[]{:S(2)}, u32[]{:S(2)}) collective-permute-start(bf16[8,2560]{1,0:T(8,128)(2,1)S(1)} %get-tuple-element.45.own_up), channel_id=1, source_target_pairs={{0,2},{1,3},{2,0},{3,1},{4,6},{5,7},{6,4},{7,5},{8,10},{9,11},{10,... | collective-permute-start | bytes 122888 | tf_op jit(solution)/shard_map/ppermute | solution.py:352
  8.7 5.0 %collective-permute-start.1 = (bf16[8,5248]{1,0:T(8,128)(2,1)S(1)}, bf16[8,5248]{1,0:T(8,128)(2,1)S(1)}, u32[]{:S(2)}, u32[]{:S(2)}) collective-permute-start(bf16[8,5248]{1,0:T(8,128)(2,1)S(1)} %pad_maximum_fusion.1), channel_id=1, source_target_pairs={{0,4},{1,5},{2,6},{3,7},{4,0},{5,1},{6,2},{7,3},{8,12},{9,13},{10,... | collective-permute-start | bytes 251912 | tf_op jit(solution)/shard_map/ppermute | solution.py:352
  13.9 9.2 %collective-permute-start.5 = (bf16[16,5248]{1,0:T(8,128)(2,1)S(1)}, bf16[16,5248]{1,0:T(8,128)(2,1)S(1)}, u32[]{:S(2)}, u32[]{:S(2)}) collective-permute-start(bf16[16,5248]{1,0:T(8,128)(2,1)S(1)} %pad_maximum_fusion.refs_7_), channel_id=1, source_target_pairs={{0,18},{1,19},{2,16},{3,17},{4,22},{5,23},{6,20},{7,21},{8,26},{9,... | collective-permute-start | bytes 503816 | tf_op jit(solution)/shard_map/ppermute | solution.py:352
  15.7 8.2 %collective-permute-start.6 = (bf16[16,5248]{1,0:T(8,128)(2,1)S(1)}, bf16[16,5248]{1,0:T(8,128)(2,1)S(1)}, u32[]{:S(2)}, u32[]{:S(2)}) collective-permute-start(bf16[16,5248]{1,0:T(8,128)(2,1)S(1)} %pad_maximum_fusion.refs_7_), channel_id=1, source_target_pairs={{0,2},{1,3},{2,0},{3,1},{4,6},{5,7},{6,4},{7,5},{8,10},{9,11},{10,... | collective-permute-start | bytes 503816 | tf_op jit(solution)/shard_map/ppermute | solution.py:352
  16.2 7.7 %collective-permute-start.7 = (bf16[16,5248]{1,0:T(8,128)(2,1)S(1)}, bf16[16,5248]{1,0:T(8,128)(2,1)S(1)}, u32[]{:S(2)}, u32[]{:S(2)}) collective-permute-start(bf16[16,5248]{1,0:T(8,128)(2,1)S(1)} %pad_maximum_fusion.refs_7_), channel_id=1, source_target_pairs={{0,16},{1,17},{2,18},{3,19},{4,20},{5,21},{6,22},{7,23},{8,24},{9,... | collective-permute-start | bytes 503816 | tf_op jit(solution)/shard_map/ppermute | solution.py:352
  17.4 7.0 %collective-permute-start.12 = (bf16[16,2560]{1,0:T(8,128)(2,1)S(1)}, bf16[16,2560]{1,0:T(8,128)(2,1)S(1)}, u32[]{:S(2)}, u32[]{:S(2)}) collective-permute-start(bf16[16,2560]{1,0:T(8,128)(2,1)S(1)} %constant_dynamic-update-slice_fusion.first_ref), channel_id=1, source_target_pairs={{0,8},{1,9},{2,10},{3,11},{4,12},{5,13},{6,14},{7,15},{8,0},{9,1},... | collective-permute-start | bytes 245768 | tf_op jit(solution)/shard_map/ppermute | solution.py:352
  19.7 5.7 %collective-permute-start.11 = (bf16[16,5248]{1,0:T(8,128)(2,1)S(1)}, bf16[16,5248]{1,0:T(8,128)(2,1)S(1)}, u32[]{:S(2)}, u32[]{:S(2)}) collective-permute-start(bf16[16,5248]{1,0:T(8,128)(2,1)S(1)} %pad_maximum_fusion.refs_7_), channel_id=1, source_target_pairs={{0,1},{1,0},{2,3},{3,2},{4,5},{5,4},{6,7},{7,6},{8,9},{9,8},{10,11... | collective-permute-start | bytes 503816 | tf_op jit(solution)/shard_map/ppermute | solution.py:352
  23.9 1.4 %collective-permute-start.8 = (bf16[16,5248]{1,0:T(8,128)(2,1)S(1)}, bf16[16,5248]{1,0:T(8,128)(2,1)S(1)}, u32[]{:S(2)}, u32[]{:S(2)}) collective-permute-start(bf16[16,5248]{1,0:T(8,128)(2,1)S(1)} %collective-permute-done.5.refs_4_), channel_id=1, source_target_pairs={{0,1},{1,0},{2,3},{3,2},{4,5},{5,4},{6,7},{7,6},{8,9},{9,8},{10,11... | collective-permute-start | bytes 503816 | tf_op jit(solution)/shard_map/ppermute | solution.py:352
  23.9 1.6 %collective-permute-start.9 = (bf16[16,5248]{1,0:T(8,128)(2,1)S(1)}, bf16[16,5248]{1,0:T(8,128)(2,1)S(1)}, u32[]{:S(2)}, u32[]{:S(2)}) collective-permute-start(bf16[16,5248]{1,0:T(8,128)(2,1)S(1)} %collective-permute-done.6.refs_5_), channel_id=1, source_target_pairs={{0,1},{1,0},{2,3},{3,2},{4,5},{5,4},{6,7},{7,6},{8,9},{9,8},{10,11... | collective-permute-start | bytes 503816 | tf_op jit(solution)/shard_map/ppermute | solution.py:352
  24.4 1.4 %collective-permute-start.10 = (bf16[16,5248]{1,0:T(8,128)(2,1)S(1)}, bf16[16,5248]{1,0:T(8,128)(2,1)S(1)}, u32[]{:S(2)}, u32[]{:S(2)}) collective-permute-start(bf16[16,5248]{1,0:T(8,128)(2,1)S(1)} %collective-permute-done.7.refs_6_), channel_id=1, source_target_pairs={{0,1},{1,0},{2,3},{3,2},{4,5},{5,4},{6,7},{7,6},{8,9},{9,8},{10,11... | collective-permute-start | bytes 503816 | tf_op jit(solution)/shard_map/ppermute | solution.py:352
  24.4 6.7 %collective-permute-start.13 = (bf16[32,2560]{1,0:T(8,128)(2,1)S(1)}, bf16[32,2560]{1,0:T(8,128)(2,1)S(1)}, u32[]{:S(2)}, u32[]{:S(2)}) collective-permute-start(bf16[32,2560]{1,0:T(8,128)(2,1)S(1)} %join.1), channel_id=1, source_target_pairs={{0,4},{1,5},{2,6},{3,7},{4,0},{5,1},{6,2},{7,3},{8,12},{9,13},{10,... | collective-permute-start | bytes 491528 | tf_op jit(solution)/shard_map/ppermute | solution.py:352
  31.1 13.0 %collective-permute-start.15 = (bf16[64,2560]{1,0:T(8,128)(2,1)S(1)}, bf16[64,2560]{1,0:T(8,128)(2,1)S(1)}, u32[]{:S(2)}, u32[]{:S(2)}) collective-permute-start(bf16[64,2560]{1,0:T(8,128)(2,1)S(1)} %constant_dynamic-update-slice_fusion.2.up_near), channel_id=1, source_target_pairs={{0,1},{1,0},{2,3},{3,2},{4,5},{5,4},{6,7},{7,6},{8,9},{9,8},{10,11... | collective-permute-start | bytes 983048 | tf_op jit(solution)/shard_map/ppermute | solution.py:352
  42.9 1.3 %collective-permute-start.14 = (bf16[16,16,128]{2,1,0:T(8,128)(2,1)S(1)}, bf16[16,16,128]{2,1,0:T(8,128)(2,1)S(1)}, u32[]{:S(2)}, u32[]{:S(2)}) collective-permute-start(bf16[16,16,128]{2,1,0:T(8,128)(2,1)S(1)} %all_to_all.5.near_ref), channel_id=1, source_target_pairs={{0,1},{1,0},{2,3},{3,2},{4,5},{5,4},{6,7},{7,6},{8,9},{9,8},{10,11... | collective-permute-start | bytes 196616 | tf_op jit(solution)/shard_map/ppermute | solution.py:352
